TPU v7x, 32 devices: a whole 2x2x4 slice. The times are simulated.
32 devices in a mesh: space: 8 (over y, x, core), band: 4 (over z).
Axes of the slice: x: 2, y: 2, z: 4, core: 2. Of those that a mesh axis runs over, the one named last changes fastest.
Arguments:
- states: bfloat16 [82944, 1024], P('space', 'band'), may hold values from -12 to 12, as said below
- potential: float32 [82944], P('space'), may hold values from 0 to 2, as said below
- cell_matrix: bfloat16 [512, 512], replicated, may hold values from -1 to 1, as said below
- cell_scale: float32 [200], P('space'), may hold values from 0.5 to 1.5
- connectivity: int32 [200, 512], P('space'), may hold values from 0 to 10367, as said below
- lower_bound: float32 [1], replicated, may hold values from 0.4 to 0.8
- upper_bound: float32 [1], replicated, may hold values from 16 to 20
Outputs:
- filtered: bfloat16 [82944, 1024], P('space', 'band')
- projected: float32 [1024, 1024], P('band', 'space')
Inputs may be any that keep to these rules, and one draw needn't show every extreme that they name: `connectivity`: each slab is a block of 5 x 5 x 1 hexahedral cells with 8 nodes along each edge, slabs stacked along the third dimension. Cell c of a slab is the cell at position (c % 5, (c // 5) % 5, c // 25), and its entry j is its node at corner offset (j % 8, (j // 8) % 8, j // 64). Nodes shared by cells get the same row. The nodes of node plane k along the third dimension have rows k * 1296 to (k + 1) * 1296 - 1 of the slab, in an order of their own. `states`: the copies of a node on a face shared by two slabs carry equal values. `potential`: the copies of a node on a face shared by two slabs carry equal values. `cell_matrix`: symmetric positive definite.
All inputs are finite; a program needn't handle non-finite values.
Results may differ from a plain program's by a relative error of at most 0.012.
The roundings to bfloat16 on the way count: a program that leaves them out, or rounds other values in their place, can miss the bound.
Values may be sent and summed in bfloat16 or wider, within the bound.
A program may use at most 128 MiB of HBM per device.

v0:
```python
import jax
import jax.numpy as jnp
from jax import lax
from jax.sharding import PartitionSpec as P

EDGE = 8
SLAB_XY = 5
SLAB_Z = 1
STEPS = 4
CELLS_DEV = 25


def with_halo(cells, sides, width):
    for axis, dim in sides:
        count = lax.axis_size(axis)
        ends = count - 1
        head = lax.slice_in_dim(cells, 0, width, axis=dim)
        tail = lax.slice_in_dim(cells, cells.shape[dim] - width, cells.shape[dim], axis=dim)
        cells = jnp.concatenate(
            [
                lax.ppermute(tail, axis, [(i, (i + 1) % count) for i in range(ends)]),
                cells,
                lax.ppermute(head, axis, [((i + 1) % count, i) for i in range(ends)]),
            ],
            axis=dim,
        )
    return cells


def settle(values):
    return lax.optimization_barrier(values.astype(jnp.bfloat16))


def plain_index():
    side_nodes = (EDGE - 1) * SLAB_XY + 1
    corner = jnp.arange(EDGE, dtype=jnp.int32)
    cell_ids = jnp.arange(CELLS_DEV, dtype=jnp.int32)
    cell_x = cell_ids % SLAB_XY
    cell_y = cell_ids // SLAB_XY % SLAB_XY
    cell_z = cell_ids // (SLAB_XY * SLAB_XY)
    index_x = cell_x[:, None, None, None] * (EDGE - 1) + corner[None, None, None, :]
    index_y = cell_y[:, None, None, None] * (EDGE - 1) + corner[None, None, :, None]
    index_z = cell_z[:, None, None, None] * (EDGE - 1) + corner[None, :, None, None]
    return ((index_z * side_nodes + index_y) * side_nodes + index_x).reshape(-1)


def cut_cells(field, axis, count):
    pieces = [
        lax.slice_in_dim(field, start * (EDGE - 1), start * (EDGE - 1) + EDGE, axis=axis)
        for start in range(count)
    ]
    return jnp.stack(pieces, axis=axis)


def fold_cells(blocks, axis, count, length):
    total = None
    for start in range(count):
        piece = lax.index_in_dim(blocks, start, axis=axis, keepdims=False)
        widths = [(0, 0)] * piece.ndim
        widths[axis] = (start * (EDGE - 1), length - start * (EDGE - 1) - EDGE)
        padded = jnp.pad(piece, widths)
        total = padded if total is None else total + padded
    return total


def local(states, potential, cell_matrix, cell_scale, connectivity, lower_bound, upper_bound):
    side_nodes = (EDGE - 1) * SLAB_XY + 1
    face_size = side_nodes * side_nodes
    layer_count = (EDGE - 1) * SLAB_Z + 1
    node_count = states.shape[0]
    columns = states.shape[1]
    ordered = jnp.zeros((node_count,), jnp.int32).at[plain_index()].set(connectivity.reshape(-1))
    start_states = states[ordered]
    potential_plane = potential[ordered]
    center = (lower_bound[0] + upper_bound[0]) * 0.5
    half_width = (upper_bound[0] - lower_bound[0]) * 0.5

    def apply_h(values):
        grid = values.reshape(layer_count, side_nodes, side_nodes, columns)
        blocks = cut_cells(grid, 0, SLAB_Z)
        blocks = cut_cells(blocks, 2, SLAB_XY)
        blocks = cut_cells(blocks, 4, SLAB_XY)
        blocks = blocks.transpose(0, 2, 4, 1, 3, 5, 6).reshape(-1, EDGE * EDGE * EDGE, columns)
        products = jnp.einsum(
            "ij,cjs->cis", cell_matrix, blocks, preferred_element_type=jnp.float32
        )
        products = products * cell_scale[:, None, None]
        products = products.reshape(SLAB_Z, SLAB_XY, SLAB_XY, EDGE, EDGE, EDGE, columns).transpose(
            0, 3, 1, 4, 2, 5, 6
        )
        summed = fold_cells(products, 4, SLAB_XY, side_nodes)
        summed = fold_cells(summed, 2, SLAB_XY, side_nodes)
        summed = fold_cells(summed, 0, SLAB_Z, layer_count)
        assembled = summed.reshape(node_count, columns)
        face_vals = jnp.stack([assembled[:face_size], assembled[node_count - face_size :]], axis=0)
        padded = with_halo(face_vals, (("space", 0),), 1)
        assembled = jnp.concatenate(
            [
                assembled[:face_size] + padded[0],
                assembled[face_size : node_count - face_size],
                assembled[node_count - face_size :] + padded[3],
            ],
            axis=0,
        )
        return assembled + potential_plane[:, None] * values.astype(jnp.float32)

    previous = start_states
    current = settle((apply_h(previous) - center * previous.astype(jnp.float32)) / half_width)
    for repeat in range(STEPS - 1):
        following = settle(
            2.0 * ((apply_h(current) - center * current.astype(jnp.float32)) / half_width)
            - previous.astype(jnp.float32)
        )
        previous, current = (current, following)
    image = settle(apply_h(current))
    position = lax.axis_index("space")
    slab_count = lax.axis_size("space")
    low_w = jnp.where(position > 0, 0.5, 1.0).astype(jnp.float32)
    up_w = jnp.where(position < slab_count - 1, 0.5, 1.0).astype(jnp.float32)
    image_f = image.astype(jnp.float32)
    weighted = settle(
        jnp.concatenate(
            [
                image_f[:face_size] * low_w,
                image_f[face_size : node_count - face_size],
                image_f[node_count - face_size :] * up_w,
            ],
            axis=0,
        )
    )
    global_count = face_size * ((EDGE - 1) * SLAB_Z * slab_count + 1)
    contract_rows = (((0,), (0,)), ((), ()))
    node_states, node_images = (
        lax.all_to_all(current, "band", split_axis=0, concat_axis=1, tiled=True),
        lax.all_to_all(weighted, "band", split_axis=0, concat_axis=1, tiled=True),
    )
    partial_matrix = lax.dot_general(
        node_states, node_images, contract_rows, preferred_element_type=jnp.float32
    )
    column_sums = lax.psum_scatter(
        partial_matrix.astype(jnp.bfloat16), "space", scatter_dimension=1, tiled=True
    )
    totals = lax.psum_scatter(column_sums, "band", scatter_dimension=0, tiled=True).astype(
        jnp.float32
    )
    filtered = jnp.zeros_like(states).at[ordered].set(current)
    return (filtered, totals / global_count)


def solution(mesh):
    placed = (P("space", "band"), P("space"), P(), P("space"), P("space", None), P(), P())
    return jax.shard_map(
        local,
        mesh=mesh,
        in_specs=placed,
        out_specs=(P("space", "band"), P("band", "space")),
        check_vma=False,
    )
```

profile of v0, /device:TPU:0, one launch (start us, length us, event | category | flops | bytes accessed | tf_op | source)
XLA Modules:
  0.0 1048.1 jit_solution(9500351240856223685)
XLA Ops:
  9.2 47.3 %scatter_custom_fusion = s32[10368]{0:T(1024)S(1)} fusion(s32[12800]{0:T(1024)S(1)} %fusion.79, s32[12800]{0:T(1024)S(1)} %reshape.269, s32[]{:T(128)} %constant.47.clone.1), kind=kCustom, calls=%fused_computation.256 | custom fusion | bytes 41476 | tf_op jit(solution)/shard_map/scatter | solution.py:72
  57.1 27.8 %gather_fusion = bf16[10368,256]{1,0:T(8,128)(2,1)} fusion(bf16[10368,256]{1,0:T(8,128)(2,1)} %param.7, s32[11264]{0:T(1024)S(1)} %pad_clamp_fusion), kind=kCustom, calls=%fused_computation | custom fusion | bytes 10658304 | tf_op jit(solution)/shard_map/gather | solution.py:73
  84.9 8.7 stack_reshape.15
  104.0 8.1 multiply_bitcast_fusion.4
  112.1 13.7 %copy.148 = f32[25,512,256]{2,1,0:T(8,128)} copy(f32[25,512,256]{1,2,0:T(8,128)} %multiply_bitcast_fusion.4) | data formatting | bytes 26214400 | tf_op jit(solution)/shard_map/mul | solution.py:87
  125.7 9.7 slice_bitcast_fusion.49
  135.4 9.7 pad_add_fusion.4
  145.1 9.3 slice_bitcast_fusion.44
  181.4 9.1 slice.434
  190.5 53.6 %gather_fusion.1 = f32[10368]{0:T(1024)S(1)} fusion(f32[10368]{0:T(1024)S(1)} %copy-done.1, s32[11264]{0:T(1024)S(1)} %pad_clamp_fusion), kind=kCustom, calls=%fused_computation.1 | custom fusion | bytes 124416 | tf_op jit(solution)/shard_map/gather | solution.py:74
  248.2 11.0 %fusion.18 = bf16[10368,256]{1,0:T(8,128)(2,1)} fusion(bf16[10368,256]{1,0:T(8,128)(2,1)} %gather_fusion, f32[1296,256]{1,0:T(8,128)S(1)} %bitcast_add_fusion.8, f32[7776,256]{1,0:T(8,128)S(1)} %copy-done.3, f32[1296,256]{1,0:T(8,128)S(1)} %bitcast_add_fusion.9, f32[]{:T(128)} %bitcast.30, f32[]{:T(128)} %bitcast.29, f32[10368]{0:T(1024)S(1)} %gather_fusion.1), kind=kLoop, calls=%fused_computation.44 | loop fusion | flops 23887872 | bytes 21275144 | tf_op jit(solution)/shard_map/convert_element_type | solution.py:31
  259.2 8.7 stack_reshape.16
  278.2 8.0 multiply_bitcast_fusion.3
  286.3 13.8 %copy.157 = f32[25,512,256]{2,1,0:T(8,128)} copy(f32[25,512,256]{1,2,0:T(8,128)} %multiply_bitcast_fusion.3) | data formatting | bytes 26214400 | tf_op jit(solution)/shard_map/mul | solution.py:87
  300.1 9.7 slice_bitcast_fusion.39
  309.8 9.7 pad_add_fusion.3
  319.5 9.3 slice_bitcast_fusion.34
  355.7 9.3 slice.460
  369.0 11.7 %fusion.7 = bf16[10368,256]{1,0:T(8,128)(2,1)} fusion(bf16[10368,256]{1,0:T(8,128)(2,1)} %gather_fusion, bf16[10368,256]{1,0:T(8,128)(2,1)} %fusion.18, f32[1296,256]{1,0:T(8,128)S(1)} %bitcast_add_fusion.6, f32[7776,256]{1,0:T(8,128)S(1)} %copy-done.6, f32[1296,256]{1,0:T(8,128)S(1)} %bitcast_add_fusion.7, f32[]{:T(128)} %bitcast.30, f32[]{:T(128)} %bitcast.29, ...), kind=kLoop, calls=%fused_computation.32 | loop fusion | flops 31850496 | bytes 26583560 | tf_op jit(solution)/shard_map/convert_element_type | solution.py:31
  380.7 8.7 stack_reshape.17
  407.8 14.0 %copy.166 = f32[25,512,256]{2,1,0:T(8,128)} copy(f32[25,512,256]{1,2,0:T(8,128)} %multiply_bitcast_fusion.2) | data formatting | bytes 26214400 | tf_op jit(solution)/shard_map/mul | solution.py:87
  421.9 9.7 slice_bitcast_fusion.29
  431.6 9.7 pad_add_fusion.2
  441.3 9.3 slice_bitcast_fusion.24
  480.3 9.3 slice.486
  493.6 11.7 %fusion.12 = bf16[10368,256]{1,0:T(8,128)(2,1)} fusion(bf16[10368,256]{1,0:T(8,128)(2,1)} %fusion.18, bf16[10368,256]{1,0:T(8,128)(2,1)} %fusion.7, f32[1296,256]{1,0:T(8,128)S(1)} %bitcast_add_fusion.4, f32[7776,256]{1,0:T(8,128)S(1)} %copy-done.7, f32[1296,256]{1,0:T(8,128)S(1)} %bitcast_add_fusion.5, f32[]{:T(128)} %bitcast.30, f32[]{:T(128)} %bitcast.29, ...), kind=kLoop, calls=%fused_computation.37 | loop fusion | flops 31850496 | bytes 26583560 | tf_op jit(solution)/shard_map/convert_element_type | solution.py:31
  505.3 8.7 stack_reshape.18
  524.3 8.0 multiply_bitcast_fusion.1
  532.4 13.8 %copy.175 = f32[25,512,256]{2,1,0:T(8,128)} copy(f32[25,512,256]{1,2,0:T(8,128)} %multiply_bitcast_fusion.1) | data formatting | bytes 26214400 | tf_op jit(solution)/shard_map/mul | solution.py:87
  546.2 9.7 slice_bitcast_fusion.19
  555.9 9.7 pad_add_fusion.1
  565.6 9.3 slice_bitcast_fusion.14
  601.8 9.3 slice.512
  615.2 11.7 %fusion.19 = bf16[10368,256]{1,0:T(8,128)(2,1)} fusion(bf16[10368,256]{1,0:T(8,128)(2,1)} %fusion.7, bf16[10368,256]{1,0:T(8,128)(2,1)} %fusion.12, f32[1296,256]{1,0:T(8,128)S(1)} %bitcast_add_fusion.2, f32[7776,256]{1,0:T(8,128)S(1)} %copy-done.5, f32[1296,256]{1,0:T(8,128)S(1)} %bitcast_add_fusion.3, f32[]{:T(128)} %bitcast.30, f32[]{:T(128)} %bitcast.29, ...), kind=kLoop, calls=%fused_computation.45 | loop fusion | flops 31850496 | bytes 26583560 | tf_op jit(solution)/shard_map/convert_element_type | solution.py:31
  626.8 8.7 stack_reshape.19
  654.0 14.0 %copy.185 = f32[25,512,256]{2,1,0:T(8,128)} copy(f32[25,512,256]{1,2,0:T(8,128)} %multiply_bitcast_fusion) | data formatting | bytes 26214400 | tf_op jit(solution)/shard_map/mul | solution.py:87
  668.0 9.7 slice_bitcast_fusion.9
  682.8 9.7 pad_add_fusion
  692.5 9.2 slice_bitcast_fusion.4
  728.7 9.3 slice.538
  742.0 9.9 fusion.17
  756.7 17.0 %pad_maximum_fusion = bf16[10368,256]{1,0:T(8,128)(2,1)} fusion(bf16[1296,256]{1,0:T(8,128)(2,1)S(1)} %get-tuple-element.63, bf16[7776,256]{1,0:T(8,128)(2,1)S(1)} %slice-done, bf16[1296,256]{1,0:T(8,128)(2,1)S(1)} %get-tuple-element.62), kind=kLoop, calls=%fused_computation.66 | loop fusion | flops 15925248 | bytes 10616832 | tf_op jit(solution)/shard_map/concatenate | solution.py:122
  773.6 26.6 %all-to-all-done = bf16[4,2592,256]{2,1,0:T(8,128)(2,1)} async-done(((bf16[4,2592,256]{2,1,0:T(8,128)(2,1)}), bf16[4,2592,256]{2,1,0:T(8,128)(2,1)}, u32[]{:S(2)}, u32[]{:S(2)}) %all-to-all-start) | async-done | bytes 5308448 | tf_op jit(solution)/shard_map/all_to_all | solution.py:134
  805.4 8.1 copy.182
  813.5 110.2 %all-to-all-done.1 = bf16[4,2592,256]{2,1,0:T(8,128)(2,1)} async-done(((bf16[4,2592,256]{2,1,0:T(8,128)(2,1)}), bf16[4,2592,256]{2,1,0:T(8,128)(2,1)}, u32[]{:S(2)}, u32[]{:S(2)}) %all-to-all-start.1) | async-done | bytes 5308448 | tf_op jit(solution)/shard_map/all_to_all | solution.py:135
  931.7 9.8 convolution_convert_fusion
  944.1 38.6 %reduce-scatter.7.cloned.1.call-done = bf16[128,1024]{1,0:T(8,128)(2,1)} async-done(((bf16[1024,1024]{1,0:T(8,128)(2,1)}), bf16[128,1024]{1,0:T(8,128)(2,1)}) %reduce-scatter.7.cloned.1.call-update) | async-done | bytes 262160
  984.5 55.0 %scatter_custom_fusion.1 = bf16[10368,256]{1,0:T(8,128)(2,1)} fusion(s32[10368]{0:T(1024)} %copy-done.19, bf16[10368,256]{1,0:T(8,128)(2,1)} %fusion.19, bf16[]{:T(256)} %constant.46.clone.1), kind=kCustom, calls=%fused_computation.67 | custom fusion | bytes 5308928 | tf_op jit(solution)/shard_map/scatter | solution.py:146
  (184 shorter events, 255.3 us)
Async XLA Ops:
  7.2 96.8 %copy-start = (bf16[512,512]{1,0:T(8,128)(2,1)S(1)}, bf16[512,512]{1,0:T(8,128)(2,1)}, u32[]{:S(2)}) copy-start(bf16[512,512]{1,0:T(8,128)(2,1)} %param.9) | copy-start | bytes 1572868
  56.5 0.6 copy-start.19
  102.8 1.2 copy-start.18
  160.4 83.8 %collective-permute-start = (f32[1,1296,256]{2,1,0:T(8,128)}, f32[1,1296,256]{2,1,0:T(8,128)}, u32[]{:S(2)}, u32[]{:S(2)}) collective-permute-start(f32[1,1296,256]{2,1,0:T(8,128)} %stack.280), channel_id=1, source_target_pairs={{0,4},{4,8},{8,12},{12,16},{16,20},{20,24},{24,28},{1,5},{5,9},{9,... | collective-permute-start | bytes 3981320 | tf_op jit(solution)/shard_map/ppermute | solution.py:21
  166.3 79.5 %collective-permute-start.1 = (f32[1,1296,256]{2,1,0:T(8,128)}, f32[1,1296,256]{2,1,0:T(8,128)}, u32[]{:S(2)}, u32[]{:S(2)}) collective-permute-start(f32[1,1296,256]{2,1,0:T(8,128)} %stack.281), channel_id=1, source_target_pairs={{4,0},{8,4},{12,8},{16,12},{20,16},{24,20},{28,24},{5,1},{9,5},{13... | collective-permute-start | bytes 3981320 | tf_op jit(solution)/shard_map/ppermute | solution.py:23
  181.4 9.1 copy-start.1
  190.5 53.6 %copy-start.9 = (f32[1296,256]{1,0:T(8,128)S(1)}, f32[1296,256]{1,0:T(8,128)}, u32[]{:S(2)}) copy-start(f32[1296,256]{1,0:T(8,128)} %slice.431) | copy-start | bytes 3981316
  190.5 55.3 %copy-start.8 = (f32[1296,256]{1,0:T(8,128)S(1)}, f32[1296,256]{1,0:T(8,128)}, u32[]{:S(2)}) copy-start(f32[1296,256]{1,0:T(8,128)} %slice.435) | copy-start | bytes 3981316
  244.1 4.1 copy-start.3
  334.8 30.1 %collective-permute-start.2 = (f32[1,1296,256]{2,1,0:T(8,128)}, f32[1,1296,256]{2,1,0:T(8,128)}, u32[]{:S(2)}, u32[]{:S(2)}) collective-permute-start(f32[1,1296,256]{2,1,0:T(8,128)} %stack.282), channel_id=1, source_target_pairs={{0,4},{4,8},{8,12},{12,16},{16,20},{20,24},{24,28},{1,5},{5,9},{9,... | collective-permute-start | bytes 3981320 | tf_op jit(solution)/shard_map/ppermute | solution.py:21
  342.4 24.2 %collective-permute-start.3 = (f32[1,1296,256]{2,1,0:T(8,128)}, f32[1,1296,256]{2,1,0:T(8,128)}, u32[]{:S(2)}, u32[]{:S(2)}) collective-permute-start(f32[1,1296,256]{2,1,0:T(8,128)} %stack.283), channel_id=1, source_target_pairs={{4,0},{8,4},{12,8},{16,12},{20,16},{24,20},{28,24},{5,1},{9,5},{13... | collective-permute-start | bytes 3981320 | tf_op jit(solution)/shard_map/ppermute | solution.py:23
  355.7 9.3 copy-start.14
  355.7 10.9 %copy-start.10 = (f32[1296,256]{1,0:T(8,128)S(1)}, f32[1296,256]{1,0:T(8,128)}, u32[]{:S(2)}) copy-start(f32[1296,256]{1,0:T(8,128)} %slice.461) | copy-start | bytes 3981316
  365.0 4.1 copy-start.6
  456.6 32.9 %collective-permute-start.4 = (f32[1,1296,256]{2,1,0:T(8,128)}, f32[1,1296,256]{2,1,0:T(8,128)}, u32[]{:S(2)}, u32[]{:S(2)}) collective-permute-start(f32[1,1296,256]{2,1,0:T(8,128)} %stack.284), channel_id=1, source_target_pairs={{0,4},{4,8},{8,12},{12,16},{16,20},{20,24},{24,28},{1,5},{5,9},{9,... | collective-permute-start | bytes 3981320 | tf_op jit(solution)/shard_map/ppermute | solution.py:21
  467.0 24.2 %collective-permute-start.5 = (f32[1,1296,256]{2,1,0:T(8,128)}, f32[1,1296,256]{2,1,0:T(8,128)}, u32[]{:S(2)}, u32[]{:S(2)}) collective-permute-start(f32[1,1296,256]{2,1,0:T(8,128)} %stack.285), channel_id=1, source_target_pairs={{4,0},{8,4},{12,8},{16,12},{20,16},{24,20},{28,24},{5,1},{9,5},{13... | collective-permute-start | bytes 3981320 | tf_op jit(solution)/shard_map/ppermute | solution.py:23
  480.3 9.3 copy-start.15
  480.3 10.9 %copy-start.11 = (f32[1296,256]{1,0:T(8,128)S(1)}, f32[1296,256]{1,0:T(8,128)}, u32[]{:S(2)}) copy-start(f32[1296,256]{1,0:T(8,128)} %slice.487) | copy-start | bytes 3981316
  489.5 4.1 copy-start.7
  580.9 30.2 %collective-permute-start.6 = (f32[1,1296,256]{2,1,0:T(8,128)}, f32[1,1296,256]{2,1,0:T(8,128)}, u32[]{:S(2)}, u32[]{:S(2)}) collective-permute-start(f32[1,1296,256]{2,1,0:T(8,128)} %stack.286), channel_id=1, source_target_pairs={{0,4},{4,8},{8,12},{12,16},{16,20},{20,24},{24,28},{1,5},{5,9},{9,... | collective-permute-start | bytes 3981320 | tf_op jit(solution)/shard_map/ppermute | solution.py:21
  588.6 24.2 %collective-permute-start.7 = (f32[1,1296,256]{2,1,0:T(8,128)}, f32[1,1296,256]{2,1,0:T(8,128)}, u32[]{:S(2)}, u32[]{:S(2)}) collective-permute-start(f32[1,1296,256]{2,1,0:T(8,128)} %stack.287), channel_id=1, source_target_pairs={{4,0},{8,4},{12,8},{16,12},{20,16},{24,20},{28,24},{5,1},{9,5},{13... | collective-permute-start | bytes 3981320 | tf_op jit(solution)/shard_map/ppermute | solution.py:23
  601.8 9.3 copy-start.16
  601.8 10.9 %copy-start.12 = (f32[1296,256]{1,0:T(8,128)S(1)}, f32[1296,256]{1,0:T(8,128)}, u32[]{:S(2)}) copy-start(f32[1296,256]{1,0:T(8,128)} %slice.513) | copy-start | bytes 3981316
  611.1 4.1 copy-start.5
  677.7 122.6 %all-to-all-start = ((bf16[4,2592,256]{2,1,0:T(8,128)(2,1)}), bf16[4,2592,256]{2,1,0:T(8,128)(2,1)}, u32[]{:S(2)}, u32[]{:S(2)}) async-start(bf16[4,2592,256]{2,1,0:T(8,128)(2,1)} %bitcast.425), calls=%async_computation | async-start | bytes 10616832 | tf_op jit(solution)/shard_map/all_to_all | solution.py:134
  707.7 30.2 %collective-permute-start.8 = (f32[1,1296,256]{2,1,0:T(8,128)}, f32[1,1296,256]{2,1,0:T(8,128)}, u32[]{:S(2)}, u32[]{:S(2)}) collective-permute-start(f32[1,1296,256]{2,1,0:T(8,128)} %stack.288), channel_id=1, source_target_pairs={{0,4},{4,8},{8,12},{12,16},{16,20},{20,24},{24,28},{1,5},{5,9},{9,... | collective-permute-start | bytes 3981320 | tf_op jit(solution)/shard_map/ppermute | solution.py:21
  715.4 24.3 %collective-permute-start.9 = (f32[1,1296,256]{2,1,0:T(8,128)}, f32[1,1296,256]{2,1,0:T(8,128)}, u32[]{:S(2)}, u32[]{:S(2)}) collective-permute-start(f32[1,1296,256]{2,1,0:T(8,128)} %stack.289), channel_id=1, source_target_pairs={{4,0},{8,4},{12,8},{16,12},{20,16},{24,20},{28,24},{5,1},{9,5},{13... | collective-permute-start | bytes 3981320 | tf_op jit(solution)/shard_map/ppermute | solution.py:23
  728.7 9.3 copy-start.17
  728.7 10.9 %copy-start.13 = (f32[1296,256]{1,0:T(8,128)S(1)}, f32[1296,256]{1,0:T(8,128)}, u32[]{:S(2)}) copy-start(f32[1296,256]{1,0:T(8,128)} %slice.539) | copy-start | bytes 3981316
  738.0 4.1 copy-start.4
  752.0 2.6 copy-start.2
  754.6 2.1 slice-start
  800.3 123.5 %all-to-all-start.1 = ((bf16[4,2592,256]{2,1,0:T(8,128)(2,1)}), bf16[4,2592,256]{2,1,0:T(8,128)(2,1)}, u32[]{:S(2)}, u32[]{:S(2)}) async-start(bf16[4,2592,256]{2,1,0:T(8,128)(2,1)} %bitcast.436), calls=%async_computation.1 | async-start | bytes 10616832 | tf_op jit(solution)/shard_map/all_to_all | solution.py:135
  805.4 177.3 %reduce-scatter.7.cloned.1.call-start = ((), (), s32[]{:S(2)}) async-start(), calls=%async_computation.5 | async-start | bytes 2359296
  944.0 95.5 %reduce-scatter.5.cloned.1.call-start = ((), (), s32[]{:S(2)}) async-start(), calls=%async_computation.4 | async-start | bytes 327680 | tf_op jit(solution)/shard_map/reduce_scatter | solution.py:143
Sparse Core Ops, SparseCore 0:
  944.2 38.4 reduce-scatter.6
  985.0 19.6 reduce-scatter.4
where the time goes:
time: 1060 us; the launch traced here: 1050 us
  local copies, waits for them, and re-layouts  567 us (53%)
  other arithmetic  195 us (18%)
  waiting for transfers between devices  175 us (17%)
  matrix products  50 us (5%)
  starting transfers between devices  43.9 us (4%)
  between operations  16.4 us (2%)
    all_to_all x1, waiting for transfers between devices, local(): lax.all_to_all(weighted, 'band', split_axis=0, concat_axis=1, tiled=True)  110 us
    squeeze x10, local copies, waits for them, and re-layouts, fold_cells(): piece = lax.index_in_dim(blocks, start, axis=axis, keepdims=False)  95 us
    add x10, other arithmetic, fold_cells(): total = padded if total is None else total + padded  83.8 us
    mul x5, local copies, waits for them, and re-layouts, apply_h(): products = products * cell_scale[:, None, None]  69.4 us
    convert_element_type x5, other arithmetic, settle(): return lax.optimization_barrier(values.astype(jnp.bfloat16))  56 us
    scatter x1, local copies, waits for them, and re-layouts, local(): filtered = jnp.zeros_like(states).at[ordered].set(current)  55 us
    gather x1, local copies, waits for them, and re-layouts, local(): potential_plane = potential[ordered]  53.6 us
    another operation x15, local copies, waits for them, and re-layouts, cut_cells(): return jnp.stack(pieces, axis=axis)  52.9 us
  transfers between devices with their start and end apart: 14, of which 3 were waited for; matrix products, arithmetic and copies ran while one was open for 28% of the time, Pallas kernels for 0%

commit v1 on v0

v1 whole, which is shorter than its diff:
```python
import functools

import jax
import jax.numpy as jnp
from jax import lax
from jax.experimental import pallas as pl
from jax.experimental.pallas import tpu as pltpu
from jax.sharding import PartitionSpec as P

EDGE = 8
SLAB_XY = 5
STEPS = 4
LANES = 128
SIDE = (EDGE - 1) * SLAB_XY + 1
FACE = SIDE * SIDE
CELLS = SLAB_XY * SLAB_XY
VMEM_BYTES = 58 * 1024 * 1024


def grid_order(connectivity):
    cells = connectivity.reshape(SLAB_XY, SLAB_XY, EDGE, EDGE, EDGE)
    main = cells[..., : EDGE - 1].transpose(2, 0, 3, 1, 4)
    main = main.reshape(EDGE, SLAB_XY, EDGE, SLAB_XY * (EDGE - 1))
    last = cells[:, SLAB_XY - 1, :, :, EDGE - 1].transpose(1, 0, 2)[..., None]
    rows = jnp.concatenate([main, last], axis=3)
    top = rows[:, :, : EDGE - 1].reshape(EDGE, SIDE - 1, SIDE)
    return jnp.concatenate([top, rows[:, SLAB_XY - 1, EDGE - 1 :]], axis=1).reshape(EDGE, FACE)


def sort_kernel(order_ref, states_ref, potential_ref, u_ref, pot_ref):
    z = pl.program_id(0)
    lane = lax.broadcasted_iota(jnp.int32, (FACE, EDGE), 1)
    column = jnp.sum(jnp.where(lane == z, order_ref[...], 0), axis=1, keepdims=True)
    hit = lax.broadcasted_iota(jnp.int32, (FACE, FACE), 1) == column
    picked = jnp.sum(jnp.where(hit, potential_ref[pl.ds(z, 1), :], 0.0), axis=1, keepdims=True)
    pot_ref[pl.ds(z, FACE, stride=EDGE), :] = jnp.broadcast_to(picked, (FACE, LANES))
    one_hot = jnp.where(hit, 1.0, 0.0).astype(jnp.bfloat16)
    rows = jnp.dot(one_hot, states_ref[...], preferred_element_type=jnp.float32)
    for h in range(u_ref.shape[0]):
        u_ref.at[h][pl.ds(z, FACE, stride=EDGE), :] = rows[:, h * LANES : (h + 1) * LANES]


def unsort_kernel(order_ref, f_ref, out_ref, wide):
    z = pl.program_id(0)
    halves = f_ref.shape[0]

    @pl.when(z == 0)
    def _():
        for h in range(halves):
            wide[h] = f_ref[h].astype(jnp.float32)

    row = order_ref[pl.ds(z, 1), :]
    hit = lax.broadcasted_iota(jnp.int32, (FACE, FACE), 0) == row
    one_hot = jnp.where(hit, 1.0, 0.0).astype(jnp.bfloat16)
    plane = jnp.concatenate(
        [wide.at[h][pl.ds(z, FACE, stride=EDGE), :] for h in range(halves)], axis=1
    ).astype(jnp.bfloat16)
    out_ref[...] = jnp.dot(one_hot, plane, preferred_element_type=jnp.float32).astype(jnp.bfloat16)


def filter_kernel(
    count, bounds_ref, scale_ref, u_hbm, pot_ref, matrix_ref, f_ref, w_ref,
    even, odd, acc, send, recv, load_sem, send_sem, recv_sem,
):
    halves = acc.shape[0]
    nodes = acc.shape[1]
    me = lax.axis_index("space")
    has_low = me > 0
    has_up = me < count - 1
    barrier = pltpu.get_barrier_semaphore()

    def greet(there, other):
        @pl.when(there)
        def _():
            pl.semaphore_signal(
                barrier, inc=1, device_id={"space": other}, device_id_type=pl.DeviceIdType.MESH
            )

    load = pltpu.make_async_copy(u_hbm, even, load_sem)
    load.start()
    greet(has_low, me - 1)
    greet(has_up, me + 1)
    pl.semaphore_wait(barrier, jnp.where(has_low, 1, 0) + jnp.where(has_up, 1, 0))
    load.wait()

    center = bounds_ref[0]
    inverse = bounds_ref[1]
    plane = lax.broadcasted_iota(jnp.int32, (EDGE, LANES), 0)
    low_w = jnp.where(has_low, 0.5, 1.0).astype(jnp.float32)
    up_w = jnp.where(has_up, 0.5, 1.0).astype(jnp.float32)
    weight = jnp.where(plane == 0, low_w, jnp.where(plane == EDGE - 1, up_w, 1.0))
    chunk = SIDE * EDGE
    weights = jnp.concatenate([weight] * SIDE, axis=0)

    def side_copy(step, h, side):
        return pltpu.make_async_remote_copy(
            src_ref=send.at[step % 2, h, side],
            dst_ref=recv.at[step % 2, h, 1 - side],
            send_sem=send_sem.at[step % 2, h, side],
            recv_sem=recv_sem.at[step % 2, h, 1 - side],
            device_id={"space": me - 1 if side == 0 else me + 1},
            device_id_type=pl.DeviceIdType.MESH,
        )

    def start_terms(u, h, shift):
        def body(i, carry):
            rows = pl.ds(pl.multiple_of(i * chunk, EDGE), chunk)
            acc[h, rows, :] = weights * (pot_ref[rows, :] - shift) * u[h, rows, :]
            return carry

        lax.fori_loop(0, SIDE, body, 0)

    def cell_rows(cell, y):
        corner = ((cell // SLAB_XY) * (EDGE - 1) + y) * SIDE + (cell % SLAB_XY) * (EDGE - 1)
        return pl.ds(pl.multiple_of(corner * EDGE, EDGE), EDGE * EDGE)

    def cells(u, h, group):
        blocks = [
            jnp.concatenate(
                [u[h, cell_rows(cell, y), :].astype(jnp.bfloat16) for y in range(EDGE)], axis=0
            )
            for cell in group
        ]
        block = blocks[0] if len(blocks) == 1 else jnp.concatenate(blocks, axis=1)
        product = jnp.dot(matrix_ref[...], block, preferred_element_type=jnp.float32)
        for place, cell in enumerate(group):
            scale = scale_ref[cell]
            for y in range(EDGE):
                part = product[y * EDGE * EDGE : (y + 1) * EDGE * EDGE, place * LANES : (place + 1) * LANES]
                acc[h, cell_rows(cell, y), :] += scale * part

    def all_cells(u, h):
        def body(i, carry):
            cells(u, h, (4 * i, 4 * i + 1))
            cells(u, h, (4 * i + 2, 4 * i + 3))
            return carry

        lax.fori_loop(0, CELLS // 4, body, 0)
        cells(u, h, (CELLS - 1,))

    def ship(step, h):
        for side, there in ((0, has_low), (1, has_up)):
            @pl.when(there)
            def _(side=side):
                rows = pl.ds(side * (EDGE - 1), FACE, stride=EDGE)
                send[step % 2, h, side] = acc.at[h][rows, :].astype(jnp.bfloat16)
                side_copy(step, h, side).start()

    def land(step, h):
        for side, there in ((0, has_low), (1, has_up)):
            @pl.when(there)
            def _(side=side):
                side_copy(step, h, side).wait_send()
                side_copy(step, h, 1 - side).wait_recv()
                rows = pl.ds(side * (EDGE - 1), FACE, stride=EDGE)
                acc.at[h][rows, :] = acc.at[h][rows, :] + recv[step % 2, h, side].astype(jnp.float32)

    def finish(step, h, fresh):
        shift = center if step < STEPS - 1 else 0.0

        def body(i, carry):
            rows = pl.ds(pl.multiple_of(i * chunk, EDGE), chunk)
            total = acc[h, rows, :] * inverse
            if step > 0:
                total = 2.0 * total - fresh[h, rows, :]
            narrow = total.astype(jnp.bfloat16)
            value = narrow.astype(jnp.float32)
            fresh[h, rows, :] = value
            acc[h, rows, :] = weights * (pot_ref[rows, :] - shift) * value
            return carry

        lax.fori_loop(0, SIDE, body, 0)
        if step == STEPS - 1:
            f_ref[h] = fresh[h].astype(jnp.bfloat16)

    fields = (even, odd)
    for h in range(halves):
        start_terms(even, h, center)
        all_cells(even, h)
        ship(0, h)
    for step in range(STEPS):
        fresh = fields[(step + 1) % 2]
        for h in range(halves):
            land(step, h)
            finish(step, h, fresh)
            all_cells(fresh, h)
            if step < STEPS - 1:
                ship(step + 1, h)
            else:
                w_ref[h] = acc[h].astype(jnp.bfloat16)


def vmem():
    return pl.BlockSpec(memory_space=pltpu.VMEM)


def smem():
    return pl.BlockSpec(memory_space=pltpu.SMEM)


def local(mesh, states, potential, cell_matrix, cell_scale, connectivity, lower_bound, upper_bound):
    nodes, columns = states.shape
    halves = columns // LANES
    slabs = lax.axis_size("space")
    bands = lax.axis_size("band")
    cell_nodes = cell_matrix.shape[0]
    order = grid_order(connectivity) - jnp.arange(EDGE, dtype=jnp.int32)[:, None] * FACE
    center = (lower_bound + upper_bound) * 0.5
    half_width = (upper_bound - lower_bound) * 0.5
    bounds = jnp.concatenate([center, 1.0 / half_width])

    number = jnp.arange(cell_nodes, dtype=jnp.int32)
    turned = (number % EDGE) * EDGE * EDGE + number // EDGE
    turn = (turned[:, None] == number[None, :]).astype(jnp.bfloat16)
    matrix = jnp.dot(turn, cell_matrix, preferred_element_type=jnp.float32).astype(jnp.bfloat16)
    matrix = jnp.dot(matrix, turn.T, preferred_element_type=jnp.float32).astype(jnp.bfloat16)

    whole = lambda *shape: pl.BlockSpec(shape, lambda z: (0,) * len(shape))
    start, pot = pl.pallas_call(
        sort_kernel,
        grid=(EDGE,),
        in_specs=[
            whole(FACE, EDGE),
            pl.BlockSpec((FACE, columns), lambda z: (z, 0)),
            whole(EDGE, FACE),
        ],
        out_specs=[whole(halves, nodes, LANES), whole(nodes, LANES)],
        out_shape=[
            jax.ShapeDtypeStruct((halves, nodes, LANES), jnp.float32),
            jax.ShapeDtypeStruct((nodes, LANES), jnp.float32),
        ],
        compiler_params=pltpu.CompilerParams(vmem_limit_bytes=VMEM_BYTES),
        name="sort_rows",
    )(order.T, states, potential.reshape(EDGE, FACE))

    dma = pltpu.SemaphoreType.DMA
    field = pltpu.VMEM((halves, nodes, LANES), jnp.float32)
    faces = pltpu.VMEM((2, halves, 2, FACE, LANES), jnp.bfloat16)
    narrow = jax.ShapeDtypeStruct((halves, nodes, LANES), jnp.bfloat16)
    filtered, image = pl.pallas_call(
        functools.partial(filter_kernel, slabs),
        in_specs=[smem(), smem(), pl.BlockSpec(memory_space=pl.ANY), vmem(), vmem()],
        out_specs=[vmem(), vmem()],
        out_shape=[narrow, narrow],
        scratch_shapes=[
            field, field, field, faces, faces,
            dma, dma((2, halves, 2)), dma((2, halves, 2)),
        ],
        compiler_params=pltpu.CompilerParams(
            collective_id=1, has_side_effects=True, vmem_limit_bytes=VMEM_BYTES
        ),
        name="filter_states",
    )(bounds, cell_scale, start, pot, matrix)

    out = pl.pallas_call(
        unsort_kernel,
        grid=(EDGE,),
        in_specs=[whole(EDGE, FACE), whole(halves, nodes, LANES)],
        out_specs=pl.BlockSpec((FACE, columns), lambda z: (z, 0)),
        out_shape=jax.ShapeDtypeStruct((nodes, columns), jnp.bfloat16),
        scratch_shapes=[field],
        compiler_params=pltpu.CompilerParams(vmem_limit_bytes=VMEM_BYTES),
        name="unsort_rows",
    )(order, filtered)

    return out, project(filtered, image, slabs, bands)


def project(filtered, image, slabs, bands):
    columns = filtered.shape[0] * LANES
    position = lax.axis_index("space")
    band = lax.axis_index("band")
    swap = position % 2 == 1
    role = jnp.where(swap, bands - 1 - band, band)
    middle = bands // 2

    def move(array, pairs):
        perm = []
        for s in range(slabs):
            for a, b in pairs:
                if s % 2:
                    a, b = bands - 1 - a, bands - 1 - b
                perm.append((s * bands + a, s * bands + b))
        return lax.ppermute(array, ("space", "band"), perm)

    rows = [filtered]
    for hop in range(1, middle + 1):
        rows.append(move(rows[-1], [(a, a + 1) for a in range(hop - 1, middle)]))
    images = [image]
    for hop in range(1, bands - middle):
        images.append(move(images[-1], [(a, a - 1) for a in range(middle + 1, bands - hop + 1)]))

    def product(f, w):
        blocks = [
            [
                lax.dot_general(f[i], w[j], (((0,), (0,)), ((), ())), preferred_element_type=jnp.float32)
                for j in range(f.shape[0])
            ]
            for i in range(f.shape[0])
        ]
        return jnp.block(blocks).astype(jnp.bfloat16)

    zero = jnp.zeros((columns, columns), jnp.bfloat16)
    grid = [[zero] * bands for _ in range(bands)]
    for up, f in enumerate(rows):
        for down, w in enumerate(images):
            block = product(f, w)
            for r in range(bands):
                a, b = r - up, r + down
                if a < 0 or b >= bands or (down and r < middle) or (up and r > middle):
                    continue
                kept = jnp.where(role == r, block, 0)
                grid[a][b] = grid[a][b] + kept
                if a != b:
                    grid[b][a] = grid[b][a] + kept.T
    plain = jnp.block(grid)
    mirrored = jnp.block([row[::-1] for row in grid[::-1]])
    partial = jnp.where(swap, mirrored, plain)
    sums = lax.psum_scatter(partial, "space", scatter_dimension=1, tiled=True)
    totals = lax.psum_scatter(sums, "band", scatter_dimension=0, tiled=True).astype(jnp.float32)
    return totals / (FACE * ((EDGE - 1) * slabs + 1))


def solution(mesh):
    placed = (P("space", "band"), P("space"), P(), P("space"), P("space", None), P(), P())
    return jax.shard_map(
        functools.partial(local, mesh),
        mesh=mesh,
        in_specs=placed,
        out_specs=(P("space", "band"), P("band", "space")),
        check_vma=False,
    )
```

time: 1060 us -> 440 us (0.42)
  local copies, waits for them, and re-layouts: 567 us -> 8.84 us
  other arithmetic: 195 us -> 29.1 us
  Pallas kernels: 0 us -> 111 us
  starting transfers between devices: 43.9 us -> 12.1 us
  matrix products: 50 us -> 77.1 us
    all_to_all x2 -> x0, waiting for transfers between devices: 137 us -> none  [the longest x1 110 us: local(): lax.all_to_all(weighted, 'band', split_axis=0, concat_axis=1, tiled=True)]
    pallas_call x0 -> x3, Pallas kernels: none -> 111 us  [the longest x1 71.5 us: local(): pl.pallas_call(functools.partial(filter_kernel, slabs), in_specs=[smem(),...]
    scatter x2 -> x0, local copies, waits for them, and re-layouts: 102 us -> none  [the longest x1 55 us: local(): filtered = jnp.zeros_like(states).at[ordered].set(current)]
    add x23 -> x1, other arithmetic: 102 us -> 0.01 us  [local(): turned = number % EDGE * EDGE * EDGE + number // EDGE]
    ppermute x10 -> x3, waiting for transfers between devices: 0.03 us -> 97.6 us  [move(): return lax.ppermute(array, ('space', 'band'), perm)]
    squeeze x10 -> x0, local copies, waits for them, and re-layouts: 95 us -> none  [fold_cells(): piece = lax.index_in_dim(blocks, start, axis=axis, keepdims=False)]
    gather x2 -> x0, local copies, waits for them, and re-layouts: 81.3 us -> none  [the longest x1 53.6 us: local(): potential_plane = potential[ordered]]
    reduce_scatter x1 -> x2, waiting for transfers between devices: 0.01 us -> 79.4 us  [the longest x1 72.8 us: project(): sums = lax.psum_scatter(partial, 'space', scatter_dimension=1, tiled=True)]
  transfers between devices with their start and end apart: 14 -> 5, of which waited for: 3 -> 3; matrix products, arithmetic and copies ran while one was open for 28% -> 12% of each run, Pallas kernels for 0% -> 3%
where the time goes in v1:
time: 440 us; the launch traced here: 431 us
  waiting for transfers between devices  177 us (40%)
  Pallas kernels  111 us (25%)
  matrix products  77.1 us (18%)
  other arithmetic  29.1 us (7%)
  between operations  16.2 us (4%)
  starting transfers between devices  12.1 us (3%)
  local copies, waits for them, and re-layouts  8.84 us (2%)
    ppermute x3, waiting for transfers between devices, move(): return lax.ppermute(array, ('space', 'band'), perm)  97.6 us
    dot_general x24, matrix products, product(): lax.dot_general(f[i], w[j], (((0,), (0,)), ((), ())), preferred_element_t...  75.5 us
    reduce_scatter x1, waiting for transfers between devices, project(): sums = lax.psum_scatter(partial, 'space', scatter_dimension=1, tiled=True)  72.8 us
    pallas_call x1, Pallas kernels, local(): pl.pallas_call(functools.partial(filter_kernel, slabs), in_specs=[smem(),...  71.5 us
    select_n x1, other arithmetic, project(): partial = jnp.where(swap, mirrored, plain)  26.3 us
    pallas_call x1, Pallas kernels, local(): pl.pallas_call(sort_kernel, grid=(EDGE,), in_specs=[whole(FACE, EDGE), pl...  24.9 us
    pallas_call x1, Pallas kernels, local(): pl.pallas_call(unsort_kernel, grid=(EDGE,), in_specs=[whole(EDGE, FACE),...  14.7 us
    ppermute x3, starting transfers between devices, move(): return lax.ppermute(array, ('space', 'band'), perm)  12 us
  transfers between devices with their start and end apart: 5, of which 3 were waited for; matrix products, arithmetic and copies ran while one was open for 12% of the time, Pallas kernels for 3%

profile of v1, /device:TPU:0, one launch (start us, length us, event | category | flops | bytes accessed | tf_op | source)
XLA Modules:
  0.0 431.4 jit_solution(6834484117947416255)
XLA Ops:
  7.2 1.3 reshape.46
  8.7 0.8 slice_reduce_fusion
  9.5 1.4 copy.208
  12.4 0.4 copy.209
  13.2 1.1 copy.212.order_ref
  14.3 0.7 reshape.50.potential_ref
  15.1 0.6 pad_maximum_fusion.2.bounds_ref
  15.7 1.6 convolution_convert_fusion.matrix_ref
  17.3 24.9 %sort_rows.1 = (f32[2,10368,128]{2,1,0:T(8,128)}, f32[10368,128]{1,0:T(8,128)}) custom-call(s32[1296,8]{1,0:T(8,128)} %copy.212.order_ref, bf16[10368,256]{1,0:T(8,128)(2,1)} %states_ref.1, f32[8,1296]{1,0:T(8,128)} %reshape.50.potential_ref), custom_call_target="tpu_custom_call" | custom-call | tf_op jit(solution)/shard_map/sort_rows/pallas_call | solution.py:219
  42.2 71.5 %filter_states.1 = (bf16[2,10368,128]{2,1,0:T(8,128)(2,1)}, bf16[2,10368,128]{2,1,0:T(8,128)(2,1)}) custom-call(f32[2]{0:T(128)} %pad_maximum_fusion.2.bounds_ref, f32[25]{0:T(128)} %scale_ref.1, f32[2,10368,128]{2,1,0:T(8,128)} %get-tuple-element.7.u_hbm, f32[10368,128]{1,0:T(8,128)} %get-tuple-element.8.pot_ref, ...), custom_call_target="tpu_custom_call" | custom-call | tf_op jit(solution)/shard_map/filter_states/pallas_call | solution.py:240
  113.7 3.1 collective-permute-start
  116.8 5.8 %collective-permute-start.1 = (bf16[2,10368,128]{2,1,0:T(8,128)(2,1)}, bf16[2,10368,128]{2,1,0:T(8,128)(2,1)}, u32[]{:S(2)}, u32[]{:S(2)}) collective-permute-start(bf16[2,10368,128]{2,1,0:T(8,128)(2,1)} %get-tuple-element.9.f_ref), channel_id=1, source_target_pairs={{0,1},{1,2},{7,6},{6,5},{8,9},{9,10},{15,14},{14,13},{16,17},{17,1... | collective-permute-start | bytes 15925256 | tf_op jit(solution)/shard_map/ppermute | solution.py:284
  122.6 3.6 fusion.66
  126.2 0.4 copy-done.1
  126.7 2.9 fusion.83
  129.5 0.4 copy-done.3
  130.0 1.0 fusion.100
  130.9 1.0 fusion.105
  132.2 3.6 fusion.60
  135.9 97.6 %collective-permute-done.1 = bf16[2,10368,128]{2,1,0:T(8,128)(2,1)} collective-permute-done((bf16[2,10368,128]{2,1,0:T(8,128)(2,1)}, bf16[2,10368,128]{2,1,0:T(8,128)(2,1)}, u32[]{:S(2)}, u32[]{:S(2)}) %collective-permute-start.1) | collective-permute-done | bytes 5308448 | tf_op jit(solution)/shard_map/ppermute | solution.py:284
  233.5 3.2 collective-permute-start.2
  236.6 3.5 fusion.63
  240.2 2.7 fusion.110
  242.9 2.7 fusion.113
  245.7 3.6 fusion.71
  249.3 3.5 fusion.88
  252.9 3.5 fusion.74
  256.4 2.7 fusion.91
  259.2 3.5 fusion.58
  262.7 3.5 fusion.59
  266.2 3.5 fusion.56
  269.6 3.5 fusion.57
  273.3 0.2 copy.242
  273.7 3.5 fusion.54
  277.2 3.7 fusion.55
  280.9 3.5 fusion.52
  284.3 3.5 fusion.53
  288.0 3.6 fusion.77
  291.6 3.5 fusion.94
  295.2 3.5 fusion.80
  298.7 2.7 fusion.97
  301.5 26.3 %maximum_select_fusion = bf16[1024,1024]{0,1:T(8,128)(2,1)} fusion(bf16[256,256]{0,1:T(8,128)(2,1)S(1)} %get-tuple-element.26, bf16[256,256]{0,1:T(8,128)(2,1)S(1)} %broadcast_select_fusion, bf16[256,256]{0,1:T(8,128)(2,1)S(1)} %copy.241, bf16[256,256]{0,1:T(8,128)(2,1)S(1)} %copy.240, bf16[256,1024]{0,1:T(8,128)(2,1)S(1)} %copy.242, ...), kind=kLoop, calls=%fused_computation.42 | loop fusion | flops 55574528 | bytes 4718593 | tf_op jit(solution)/shard_map/jit(_where)/select_n | solution.py:318
  327.9 72.8 %reduce-scatter.3.cloned.1.call-done = bf16[1024,128]{0,1:T(8,128)(2,1)} async-done(((bf16[1024,1024]{0,1:T(8,128)(2,1)}), bf16[1024,128]{0,1:T(8,128)(2,1)}) %reduce-scatter.3.cloned.1.call-update) | async-done | bytes 262160 | tf_op jit(solution)/shard_map/reduce_scatter | solution.py:319
  400.7 0.7 broadcast_subtract_fusion.order_ref
  401.3 14.7 %unsort_rows.1 = bf16[10368,256]{1,0:T(8,128)(2,1)} custom-call(s32[8,1296]{1,0:T(8,128)} %broadcast_subtract_fusion.order_ref, bf16[2,10368,128]{2,1,0:T(8,128)(2,1)} %get-tuple-element.9.f_ref), custom_call_target="tpu_custom_call" | custom-call | tf_op jit(solution)/shard_map/unsort_rows/pallas_call | solution.py:255
  416.1 6.6 %reduce-scatter.5.cloned.1.call-done = bf16[256,128]{0,1:T(8,128)(2,1)} async-done(((bf16[1024,128]{0,1:T(8,128)(2,1)}), bf16[256,128]{0,1:T(8,128)(2,1)}) %reduce-scatter.5.cloned.1.call-update) | async-done | bytes 65552 | tf_op jit(solution)/shard_map/reduce_scatter | solution.py:320
  422.7 0.9 convert_multiply_fusion
  423.6 0.8 copy.247
  (54 shorter events, 2.0 us)
Async XLA Ops:
  7.2 8.5 %copy-start = (bf16[512,512]{1,0:T(8,128)(2,1)S(1)}, bf16[512,512]{1,0:T(8,128)(2,1)}, u32[]{:S(2)}) copy-start(bf16[512,512]{1,0:T(8,128)(2,1)} %param.25) | copy-start | bytes 1572868
  7.2 393.4 %reduce-scatter.3.cloned.1.call-start = ((), (), s32[]{:S(2)}) async-start(), calls=%async_computation.2 | async-start | bytes 2359296 | tf_op jit(solution)/shard_map/reduce_scatter | solution.py:319
  8.6 5.8 %copy-start.2 = (f32[10368]{0:T(1024)S(1)}, f32[10368]{0:T(1024)}, u32[]{:S(2)}) copy-start(f32[10368]{0:T(1024)} %param.24) | copy-start | bytes 124420
  113.7 18.5 %collective-permute-start = (bf16[2,10368,128]{2,1,0:T(8,128)(2,1)}, bf16[2,10368,128]{2,1,0:T(8,128)(2,1)}, u32[]{:S(2)}, u32[]{:S(2)}) collective-permute-start(bf16[2,10368,128]{2,1,0:T(8,128)(2,1)} %get-tuple-element.10), channel_id=1, source_target_pairs={{3,2},{4,5},{11,10},{12,13},{19,18},{20,21},{27,26},{28,29}} | collective-permute-start | bytes 15925256 | tf_op jit(solution)/shard_map/ppermute | solution.py:284
  116.8 116.7 %collective-permute-start.1 = (bf16[2,10368,128]{2,1,0:T(8,128)(2,1)}, bf16[2,10368,128]{2,1,0:T(8,128)(2,1)}, u32[]{:S(2)}, u32[]{:S(2)}) collective-permute-start(bf16[2,10368,128]{2,1,0:T(8,128)(2,1)} %get-tuple-element.9.f_ref), channel_id=1, source_target_pairs={{0,1},{1,2},{7,6},{6,5},{8,9},{9,10},{15,14},{14,13},{16,17},{17,1... | collective-permute-start | bytes 15925256 | tf_op jit(solution)/shard_map/ppermute | solution.py:284
  122.6 4.1 copy-start.1
  126.7 3.3 copy-start.3
  132.1 108.1 %slice-start = ((s8[5308416]{0:T(1024)(128)(4,1)}), s8[1114112]{0:T(1024)(128)(4,1)S(1)}, s32[]{:S(2)}) async-start(s8[5308416]{0:T(1024)(128)(4,1)} %bitcast.176), calls=%async_computation.4 | async-start | bytes 2228224
  132.2 107.9 %slice-start.1 = ((s8[5308416]{0:T(1024)(128)(4,1)}), s8[4194304]{0:T(1024)(128)(4,1)S(1)}, s32[]{:S(2)}) async-start(s8[5308416]{0:T(1024)(128)(4,1)} %bitcast.176), calls=%async_computation.5 | async-start | bytes 8388608
  233.5 40.2 %collective-permute-start.2 = (bf16[2,10368,128]{2,1,0:T(8,128)(2,1)}, bf16[2,10368,128]{2,1,0:T(8,128)(2,1)}, u32[]{:S(2)}, u32[]{:S(2)}) collective-permute-start(bf16[2,10368,128]{2,1,0:T(8,128)(2,1)} %collective-permute-done.1), channel_id=1, source_target_pairs={{1,2},{6,5},{9,10},{14,13},{17,18},{22,21},{25,26},{30,29}} | collective-permute-start | bytes 15925256 | tf_op jit(solution)/shard_map/ppermute | solution.py:284
  245.7 10.6 %slice-start.2 = ((s8[5308416]{0:T(1024)(128)(4,1)}), s8[4194304]{0:T(1024)(128)(4,1)S(1)}, s32[]{:S(2)}) async-start(s8[5308416]{0:T(1024)(128)(4,1)} %bitcast.187), calls=%async_computation.6 | async-start | bytes 8388608
  249.3 7.0 %slice-start.3 = ((s8[5308416]{0:T(1024)(128)(4,1)}), s8[1114112]{0:T(1024)(128)(4,1)S(1)}, s32[]{:S(2)}) async-start(s8[5308416]{0:T(1024)(128)(4,1)} %bitcast.187), calls=%async_computation.7 | async-start | bytes 2228224
  288.0 10.6 %slice-start.4 = ((s8[5308416]{0:T(1024)(128)(4,1)}), s8[4194304]{0:T(1024)(128)(4,1)S(1)}, s32[]{:S(2)}) async-start(s8[5308416]{0:T(1024)(128)(4,1)} %bitcast.189), calls=%async_computation.8 | async-start | bytes 8388608
  291.6 7.0 %slice-start.5 = ((s8[5308416]{0:T(1024)(128)(4,1)}), s8[1114112]{0:T(1024)(128)(4,1)S(1)}, s32[]{:S(2)}) async-start(s8[5308416]{0:T(1024)(128)(4,1)} %bitcast.189), calls=%async_computation.9 | async-start | bytes 2228224
  327.8 94.9 %reduce-scatter.5.cloned.1.call-start = ((), (), s32[]{:S(2)}) async-start(), calls=%async_computation.3 | async-start | bytes 327680 | tf_op jit(solution)/shard_map/reduce_scatter | solution.py:320
Sparse Core Ops, SparseCore 0:
  327.9 72.6 reduce-scatter.2
  403.0 19.6 reduce-scatter.4

commit v2 on v1

--- a/solution.py
+++ b/solution.py
@@ -42,12 +42,12 @@
 
 def unsort_kernel(order_ref, f_ref, out_ref, wide):
     z = pl.program_id(0)
-    halves = f_ref.shape[0]
+    halves = wide.shape[0]
 
     @pl.when(z == 0)
     def _():
         for h in range(halves):
-            wide[h] = f_ref[h].astype(jnp.float32)
+            wide[h] = f_ref[:, h * LANES : (h + 1) * LANES].astype(jnp.float32)
 
     row = order_ref[pl.ds(z, 1), :]
     hit = lax.broadcasted_iota(jnp.int32, (FACE, FACE), 0) == row
@@ -171,7 +171,7 @@
 
         lax.fori_loop(0, SIDE, body, 0)
         if step == STEPS - 1:
-            f_ref[h] = fresh[h].astype(jnp.bfloat16)
+            f_ref[:, h * LANES : (h + 1) * LANES] = fresh[h].astype(jnp.bfloat16)
 
     fields = (even, odd)
     for h in range(halves):
@@ -187,7 +187,7 @@
             if step < STEPS - 1:
                 ship(step + 1, h)
             else:
-                w_ref[h] = acc[h].astype(jnp.bfloat16)
+                w_ref[:, h * LANES : (h + 1) * LANES] = acc[h].astype(jnp.bfloat16)
 
 
 def vmem():
@@ -236,7 +236,7 @@
     dma = pltpu.SemaphoreType.DMA
     field = pltpu.VMEM((halves, nodes, LANES), jnp.float32)
     faces = pltpu.VMEM((2, halves, 2, FACE, LANES), jnp.bfloat16)
-    narrow = jax.ShapeDtypeStruct((halves, nodes, LANES), jnp.bfloat16)
+    narrow = jax.ShapeDtypeStruct((nodes, columns), jnp.bfloat16)
     filtered, image = pl.pallas_call(
         functools.partial(filter_kernel, slabs),
         in_specs=[smem(), smem(), pl.BlockSpec(memory_space=pl.ANY), vmem(), vmem()],
@@ -252,26 +252,115 @@
         name="filter_states",
     )(bounds, cell_scale, start, pot, matrix)
 
-    out = pl.pallas_call(
+    unsort = pl.pallas_call(
         unsort_kernel,
         grid=(EDGE,),
-        in_specs=[whole(EDGE, FACE), whole(halves, nodes, LANES)],
+        in_specs=[whole(EDGE, FACE), whole(nodes, columns)],
         out_specs=pl.BlockSpec((FACE, columns), lambda z: (z, 0)),
         out_shape=jax.ShapeDtypeStruct((nodes, columns), jnp.bfloat16),
         scratch_shapes=[field],
         compiler_params=pltpu.CompilerParams(vmem_limit_bytes=VMEM_BYTES),
+        cost_estimate=pl.CostEstimate(
+            flops=2 * nodes * FACE * columns, bytes_accessed=4 * nodes * columns, transcendentals=0
+        ),
         name="unsort_rows",
-    )(order, filtered)
-
-    return out, project(filtered, image, slabs, bands)
-
-
-def project(filtered, image, slabs, bands):
-    columns = filtered.shape[0] * LANES
-    position = lax.axis_index("space")
+    )
+    return project(filtered, image, slabs, bands, lambda: unsort(order, filtered))
+
+
+def held_by(up, down, bands):
+    middle = bands // 2
+    first = middle if down else up
+    last = middle if up else bands - 1 - down
+    return first, last
+
+
+def combine_kernel(slabs, bands, ups, downs, *refs):
+    f_refs, w_refs = refs[:ups], refs[ups : ups + downs]
+    out_ref, acc, whole, landed, send_sem, recv_sem = refs[ups + downs :]
+    step = pl.program_id(0)
+    width = acc.shape[-1]
+    rows = whole.shape[0] // slabs
+    me = lax.axis_index("space")
     band = lax.axis_index("band")
-    swap = position % 2 == 1
+    swap = lax.rem(me, 2) == 1
     role = jnp.where(swap, bands - 1 - band, band)
+    barrier = pltpu.get_barrier_semaphore()
+
+    @pl.when(step == 0)
+    def _():
+        for d in range(1, slabs):
+            pl.semaphore_signal(
+                barrier,
+                inc=1,
+                device_id={"space": lax.rem(me + d, slabs)},
+                device_id_type=pl.DeviceIdType.MESH,
+            )
+        acc[...] = jnp.zeros_like(acc)
+
+    for up in range(ups):
+        for down in range(downs):
+            first, last = held_by(up, down, bands)
+
+            @pl.when((role >= first) & (role <= last))
+            def _(up=up, down=down):
+                acc[up, down] += lax.dot_general(
+                    f_refs[up][...],
+                    w_refs[down][...],
+                    (((0,), (0,)), ((), ())),
+                    preferred_element_type=jnp.float32,
+                )
+
+    @pl.when(step == pl.num_programs(0) - 1)
+    def _():
+        whole[...] = jnp.zeros_like(whole)
+        for mirrored in range(2):
+            for up in range(ups):
+                for down in range(downs):
+                    first, last = held_by(up, down, bands)
+                    for r in range(first, last + 1):
+                        a, b = r - up, r + down
+                        if mirrored:
+                            a, b = bands - 1 - a, bands - 1 - b
+
+                        @pl.when((role == r) & (swap if mirrored else jnp.logical_not(swap)))
+                        def _(up=up, down=down, a=a, b=b):
+                            block = acc[up, down]
+                            whole[a * width : (a + 1) * width, b * width : (b + 1) * width] = block.astype(
+                                jnp.bfloat16
+                            )
+                            if a != b:
+                                whole[b * width : (b + 1) * width, a * width : (a + 1) * width] = (
+                                    block.T.astype(jnp.bfloat16)
+                                )
+
+        pl.semaphore_wait(barrier, slabs - 1)
+        copies = []
+        for d in range(1, slabs):
+            peer = lax.rem(me + d, slabs)
+            copies.append(
+                pltpu.make_async_remote_copy(
+                    src_ref=whole.at[pl.ds(pl.multiple_of(peer * rows, rows), rows), :],
+                    dst_ref=landed.at[d - 1],
+                    send_sem=send_sem.at[d - 1],
+                    recv_sem=recv_sem.at[d - 1],
+                    device_id={"space": peer},
+                    device_id_type=pl.DeviceIdType.MESH,
+                )
+            )
+        for copy in copies:
+            copy.start()
+        total = whole[pl.ds(pl.multiple_of(me * rows, rows), rows), :].astype(jnp.float32)
+        for d, copy in enumerate(copies):
+            copy.wait_recv()
+            total = total + landed[d].astype(jnp.float32)
+        out_ref[...] = total.astype(jnp.bfloat16)
+        for copy in copies:
+            copy.wait_send()
+
+
+def project(filtered, image, slabs, bands, unsort):
+    nodes, columns = filtered.shape
     middle = bands // 2
 
     def move(array, pairs):
@@ -283,42 +372,38 @@
                 perm.append((s * bands + a, s * bands + b))
         return lax.ppermute(array, ("space", "band"), perm)
 
-    rows = [filtered]
-    for hop in range(1, middle + 1):
+    rows = [filtered, move(filtered, [(a, a + 1) for a in range(middle)])]
+    out, rows[-1], image = lax.optimization_barrier((unsort(), rows[-1], image))
+    for hop in range(2, middle + 1):
         rows.append(move(rows[-1], [(a, a + 1) for a in range(hop - 1, middle)]))
     images = [image]
     for hop in range(1, bands - middle):
         images.append(move(images[-1], [(a, a - 1) for a in range(middle + 1, bands - hop + 1)]))
 
-    def product(f, w):
-        blocks = [
-            [
-                lax.dot_general(f[i], w[j], (((0,), (0,)), ((), ())), preferred_element_type=jnp.float32)
-                for j in range(f.shape[0])
-            ]
-            for i in range(f.shape[0])
-        ]
-        return jnp.block(blocks).astype(jnp.bfloat16)
-
-    zero = jnp.zeros((columns, columns), jnp.bfloat16)
-    grid = [[zero] * bands for _ in range(bands)]
-    for up, f in enumerate(rows):
-        for down, w in enumerate(images):
-            block = product(f, w)
-            for r in range(bands):
-                a, b = r - up, r + down
-                if a < 0 or b >= bands or (down and r < middle) or (up and r > middle):
-                    continue
-                kept = jnp.where(role == r, block, 0)
-                grid[a][b] = grid[a][b] + kept
-                if a != b:
-                    grid[b][a] = grid[b][a] + kept.T
-    plain = jnp.block(grid)
-    mirrored = jnp.block([row[::-1] for row in grid[::-1]])
-    partial = jnp.where(swap, mirrored, plain)
-    sums = lax.psum_scatter(partial, "space", scatter_dimension=1, tiled=True)
-    totals = lax.psum_scatter(sums, "band", scatter_dimension=0, tiled=True).astype(jnp.float32)
-    return totals / (FACE * ((EDGE - 1) * slabs + 1))
+    ups, downs = len(rows), len(images)
+    states = bands * columns
+    share = states // slabs
+    dma = pltpu.SemaphoreType.DMA
+    sums = pl.pallas_call(
+        functools.partial(combine_kernel, slabs, bands, ups, downs),
+        grid=(EDGE,),
+        in_specs=[pl.BlockSpec((nodes // EDGE, columns), lambda z: (z, 0))] * (ups + downs),
+        out_specs=pl.BlockSpec((share, states), lambda z: (0, 0)),
+        out_shape=jax.ShapeDtypeStruct((share, states), jnp.bfloat16),
+        scratch_shapes=[
+            pltpu.VMEM((ups, downs, columns, columns), jnp.float32),
+            pltpu.VMEM((states, states), jnp.bfloat16),
+            pltpu.VMEM((slabs - 1, share, states), jnp.bfloat16),
+            dma((slabs - 1,)),
+            dma((slabs - 1,)),
+        ],
+        compiler_params=pltpu.CompilerParams(
+            collective_id=2, has_side_effects=True, vmem_limit_bytes=VMEM_BYTES
+        ),
+        name="combine",
+    )(*rows, *images)
+    totals = lax.psum_scatter(sums, "band", scatter_dimension=1, tiled=True).astype(jnp.float32)
+    return out, totals.T / (FACE * ((EDGE - 1) * slabs + 1))
 
 
 def solution(mesh):

time: 440 us -> 314 us (0.71); the launches traced: 431 us -> 314 us
  waiting for transfers between devices: 177 us -> 71.2 us
  Pallas kernels: 111 us -> 204 us
  matrix products: 77.1 us -> 1.63 us
  other arithmetic: 29.1 us -> 2.41 us
    pallas_call x1 -> x2, Pallas kernels: 14.7 us -> 108 us  [the longest x1 92.9 us: project(): pl.pallas_call(functools.partial(combine_kernel, slabs, bands, ups, downs...]
    dot_general x24 -> x0, matrix products: 75.5 us -> none  [product(): lax.dot_general(f[i], w[j], (((0,), (0,)), ((), ())), preferred_element_t...]
    ppermute x3, waiting for transfers between devices: 97.6 us -> 40.4 us  [move(): return lax.ppermute(array, ('space', 'band'), perm)]
    reduce_scatter x2 -> x1, waiting for transfers between devices: 79.4 us -> 30.8 us  [project(): lax.psum_scatter(sums, 'band', scatter_dimension=1, tiled=True)]
    select_n x9 -> x0, other arithmetic: 26.5 us -> none  [the longest x1 26.3 us: project(): partial = jnp.where(swap, mirrored, plain)]
  transfers between devices with their start and end apart: 5 -> 4, of which waited for: 3 -> 2; matrix products, arithmetic and copies ran while one was open for 12% -> 0% of each run, Pallas kernels for 3% -> 5%
where the time goes in v2:
time: 314 us
  Pallas kernels  204 us (65%)
  waiting for transfers between devices  71.2 us (23%)
  between operations  15.5 us (5%)
  starting transfers between devices  11.9 us (4%)
  local copies, waits for them, and re-layouts  6.86 us (2%)
    pallas_call x1, Pallas kernels, project(): pl.pallas_call(functools.partial(combine_kernel, slabs, bands, ups, downs...  92.9 us
    pallas_call x1, Pallas kernels, local(): pl.pallas_call(functools.partial(filter_kernel, slabs), in_specs=[smem(),...  71.6 us
    ppermute x3, waiting for transfers between devices, move(): return lax.ppermute(array, ('space', 'band'), perm)  40.4 us
    reduce_scatter x1, waiting for transfers between devices, project(): lax.psum_scatter(sums, 'band', scatter_dimension=1, tiled=True)  30.8 us
    pallas_call x1, Pallas kernels, local(): pl.pallas_call(sort_kernel, grid=(EDGE,), in_specs=[whole(FACE, EDGE), pl...  24.8 us
    pallas_call x1, Pallas kernels, local(): unsort(order, filtered)  14.9 us
    ppermute x3, starting transfers between devices, move(): return lax.ppermute(array, ('space', 'band'), perm)  11.9 us
  transfers between devices with their start and end apart: 4, of which 2 were waited for; matrix products, arithmetic and copies ran while one was open for 0% of the time, Pallas kernels for 5%

profile of v2, /device:TPU:0, one launch (start us, length us, event | category | flops | bytes accessed | tf_op | source)
XLA Modules:
  0.0 313.7 jit_solution(13768225777195797235)
XLA Ops:
  7.2 0.0 copy-start
  7.2 0.0 copy-start.2
  7.2 0.0 reduce-scatter.2.cloned.1.call-start
  8.6 1.3 reshape.46
  9.9 0.8 slice_reduce_fusion
  10.7 0.1 slice_bitcast_fusion
  10.8 1.4 copy.38
  12.2 0.1 pad_add_fusion
  12.4 0.1 slice_add_fusion
  12.4 0.0 copy-done.2
  12.4 0.7 reshape.50.potential_ref
  13.2 0.1 copy.40
  13.3 0.4 copy.39
  13.8 0.1 reshape.49
  13.9 0.1 fusion.12
  13.9 1.1 copy.42.order_ref
  15.1 0.6 pad_maximum_fusion.bounds_ref
  15.7 0.0 copy-done
  15.7 1.6 convolution_convert_fusion.matrix_ref
  17.3 24.8 %sort_rows.1 = (f32[2,10368,128]{2,1,0:T(8,128)}, f32[10368,128]{1,0:T(8,128)}) custom-call(s32[1296,8]{1,0:T(8,128)} %copy.42.order_ref, bf16[10368,256]{1,0:T(8,128)(2,1)} %states_ref.1, f32[8,1296]{1,0:T(8,128)} %reshape.50.potential_ref), custom_call_target="tpu_custom_call" | custom-call | tf_op jit(solution)/shard_map/sort_rows/pallas_call | solution.py:219
  42.1 71.6 %filter_states.1 = (bf16[10368,256]{1,0:T(8,128)(2,1)}, bf16[10368,256]{1,0:T(8,128)(2,1)}) custom-call(f32[2]{0:T(128)} %pad_maximum_fusion.bounds_ref, f32[25]{0:T(128)} %scale_ref.1, f32[2,10368,128]{2,1,0:T(8,128)} %get-tuple-element.9.u_hbm, f32[10368,128]{1,0:T(8,128)} %get-tuple-element.10.pot_ref, bf16[512,512]{1,0:T(8,128)(2,1)} %convolution_convert_fusion.matrix_ref), custom_call_target="tpu_custom_call" | custom-call | tf_op jit(solution)/shard_map/filter_states/pallas_call | solution.py:240
  113.7 5.8 %collective-permute-start = (bf16[10368,256]{1,0:T(8,128)(2,1)}, bf16[10368,256]{1,0:T(8,128)(2,1)}, u32[]{:S(2)}, u32[]{:S(2)}) collective-permute-start(bf16[10368,256]{1,0:T(8,128)(2,1)} %get-tuple-element.11.f_ref.refs_0_), channel_id=1, source_target_pairs={{0,1},{1,2},{7,6},{6,5},{8,9},{9,10},{15,14},{14,13},{16,17},{17,1... | collective-permute-start | bytes 15925256 | tf_op jit(solution)/shard_map/ppermute | solution.py:373
  119.5 0.7 broadcast_subtract_fusion.order_ref
  120.2 0.0 copy-start.1
  120.2 14.9 %unsort_rows.1 = bf16[10368,256]{1,0:T(8,128)(2,1)} custom-call(s32[8,1296]{1,0:T(8,128)} %broadcast_subtract_fusion.order_ref, bf16[10368,256]{1,0:T(8,128)(2,1)} %get-tuple-element.11.f_ref.refs_0_), custom_call_target="tpu_custom_call" | custom-call | flops 6879707136 | bytes 10616832 | tf_op jit(solution)/shard_map/unsort_rows/pallas_call | solution.py:268
  135.1 40.4 %collective-permute-done.refs_1_ = bf16[10368,256]{1,0:T(8,128)(2,1)} collective-permute-done((bf16[10368,256]{1,0:T(8,128)(2,1)}, bf16[10368,256]{1,0:T(8,128)(2,1)}, u32[]{:S(2)}, u32[]{:S(2)}) %collective-permute-start) | collective-permute-done | bytes 5308448 | tf_op jit(solution)/shard_map/ppermute | solution.py:373
  175.5 3.0 collective-permute-start.1
  178.5 0.0 copy-done.1
  178.5 3.0 collective-permute-start.2
  181.5 0.0 collective-permute-done.1.refs_2_
  181.5 0.0 collective-permute-done.2.refs_4_
  181.5 92.9 %combine.1 = bf16[128,1024]{1,0:T(8,128)(2,1)} custom-call(bf16[10368,256]{1,0:T(8,128)(2,1)} %get-tuple-element.11.f_ref.refs_0_, bf16[10368,256]{1,0:T(8,128)(2,1)} %collective-permute-done.refs_1_, bf16[10368,256]{1,0:T(8,128)(2,1)} %collective-permute-done.1.refs_2_, bf16[10368,256]{1,0:T(8,128)(2,1)} %get-tuple-element.15.refs_3_, ...), custom_call_target="tpu_custom_call" | custom-call | tf_op jit(solution)/shard_map/combine/pallas_call | solution.py:387
  274.4 0.0 reduce-scatter.2.cloned.1.call-update
  274.4 30.8 %reduce-scatter.2.cloned.1.call-done = bf16[128,256]{1,0:T(8,128)(2,1)} async-done(((bf16[128,1024]{1,0:T(8,128)(2,1)}), bf16[128,256]{1,0:T(8,128)(2,1)}) %reduce-scatter.2.cloned.1.call-update) | async-done | bytes 65552 | tf_op jit(solution)/shard_map/reduce_scatter | solution.py:405
  305.2 0.9 multiply_bitcast_fusion
  306.1 0.8 copy.43
  (4 shorter events, 0.1 us)
Async XLA Ops:
  7.2 8.5 %copy-start = (bf16[512,512]{1,0:T(8,128)(2,1)S(1)}, bf16[512,512]{1,0:T(8,128)(2,1)}, u32[]{:S(2)}) copy-start(bf16[512,512]{1,0:T(8,128)(2,1)} %param.9) | copy-start | bytes 1572868
  7.2 5.3 %copy-start.2 = (f32[10368]{0:T(1024)S(1)}, f32[10368]{0:T(1024)}, u32[]{:S(2)}) copy-start(f32[10368]{0:T(1024)} %param.8) | copy-start | bytes 124420
  7.2 298.1 %reduce-scatter.2.cloned.1.call-start = ((), (), s32[]{:S(2)}) async-start(), calls=%async_computation.1 | async-start | bytes 327680 | tf_op jit(solution)/shard_map/reduce_scatter | solution.py:405
  113.7 61.7 %collective-permute-start = (bf16[10368,256]{1,0:T(8,128)(2,1)}, bf16[10368,256]{1,0:T(8,128)(2,1)}, u32[]{:S(2)}, u32[]{:S(2)}) collective-permute-start(bf16[10368,256]{1,0:T(8,128)(2,1)} %get-tuple-element.11.f_ref.refs_0_), channel_id=1, source_target_pairs={{0,1},{1,2},{7,6},{6,5},{8,9},{9,10},{15,14},{14,13},{16,17},{17,1... | collective-permute-start | bytes 15925256 | tf_op jit(solution)/shard_map/ppermute | solution.py:373
  120.2 58.3 %copy-start.1 = (bf16[10368,256]{1,0:T(8,128)(2,1)S(1)}, bf16[10368,256]{1,0:T(8,128)(2,1)}, u32[]{:S(2)}) copy-start(bf16[10368,256]{1,0:T(8,128)(2,1)} %get-tuple-element.15.refs_3_) | copy-start | bytes 15925252
  175.5 6.1 %collective-permute-start.1 = (bf16[10368,256]{1,0:T(8,128)(2,1)}, bf16[10368,256]{1,0:T(8,128)(2,1)}, u32[]{:S(2)}, u32[]{:S(2)}) collective-permute-start(bf16[10368,256]{1,0:T(8,128)(2,1)} %collective-permute-done.refs_1_), channel_id=1, source_target_pairs={{1,2},{6,5},{9,10},{14,13},{17,18},{22,21},{25,26},{30,29}} | collective-permute-start | bytes 15925256 | tf_op jit(solution)/shard_map/ppermute | solution.py:373
  178.5 3.0 collective-permute-start.2
Sparse Core Ops, SparseCore 0:
  274.6 30.6 reduce-scatter.1

commit v3 on v2

--- a/solution.py
+++ b/solution.py
@@ -275,11 +275,11 @@
     return first, last
 
 
-def combine_kernel(slabs, bands, ups, downs, *refs):
+def combine_kernel(slabs, bands, ups, downs, nodes_all, *refs):
     f_refs, w_refs = refs[:ups], refs[ups : ups + downs]
-    out_ref, acc, whole, landed, send_sem, recv_sem = refs[ups + downs :]
+    out_ref, acc, whole, landed, mine, got, send_sem, recv_sem, band_send, band_recv = refs[ups + downs :]
     step = pl.program_id(0)
-    width = acc.shape[-1]
+    width = acc.shape[1]
     rows = whole.shape[0] // slabs
     me = lax.axis_index("space")
     band = lax.axis_index("band")
@@ -289,52 +289,53 @@
 
     @pl.when(step == 0)
     def _():
-        for d in range(1, slabs):
-            pl.semaphore_signal(
-                barrier,
-                inc=1,
-                device_id={"space": lax.rem(me + d, slabs)},
-                device_id_type=pl.DeviceIdType.MESH,
-            )
+        for axis, place, count in (("space", me, slabs), ("band", band, bands)):
+            for d in range(1, count):
+                pl.semaphore_signal(
+                    barrier,
+                    inc=1,
+                    device_id={axis: lax.rem(place + d, count)},
+                    device_id_type=pl.DeviceIdType.MESH,
+                )
         acc[...] = jnp.zeros_like(acc)
 
-    for up in range(ups):
-        for down in range(downs):
-            first, last = held_by(up, down, bands)
-
-            @pl.when((role >= first) & (role <= last))
-            def _(up=up, down=down):
-                acc[up, down] += lax.dot_general(
-                    f_refs[up][...],
-                    w_refs[down][...],
-                    (((0,), (0,)), ((), ())),
-                    preferred_element_type=jnp.float32,
+    held = {}
+    for r in range(bands):
+        for up in range(ups):
+            for down in range(downs):
+                first, last = held_by(up, down, bands)
+                if first <= r <= last:
+                    held.setdefault(r, {}).setdefault(down, []).append(up)
+
+    for r, images in held.items():
+        @pl.when(role == r)
+        def _(images=images):
+            for down, fields in images.items():
+                sides = [f_refs[up][...] for up in fields]
+                side = sides[0] if len(sides) == 1 else jnp.concatenate(sides, axis=1)
+                acc[down, :, : len(fields) * width] += lax.dot_general(
+                    w_refs[down][...], side, (((0,), (0,)), ((), ())), preferred_element_type=jnp.float32
                 )
 
     @pl.when(step == pl.num_programs(0) - 1)
     def _():
         whole[...] = jnp.zeros_like(whole)
         for mirrored in range(2):
-            for up in range(ups):
-                for down in range(downs):
-                    first, last = held_by(up, down, bands)
-                    for r in range(first, last + 1):
-                        a, b = r - up, r + down
-                        if mirrored:
-                            a, b = bands - 1 - a, bands - 1 - b
-
-                        @pl.when((role == r) & (swap if mirrored else jnp.logical_not(swap)))
-                        def _(up=up, down=down, a=a, b=b):
-                            block = acc[up, down]
-                            whole[a * width : (a + 1) * width, b * width : (b + 1) * width] = block.astype(
-                                jnp.bfloat16
-                            )
+            for r, images in held.items():
+                @pl.when((role == r) & (swap if mirrored else jnp.logical_not(swap)))
+                def _(mirrored=mirrored, r=r, images=images):
+                    for down, fields in images.items():
+                        for up in fields:
+                            a, b = r - up, r + down
+                            if mirrored:
+                                a, b = bands - 1 - a, bands - 1 - b
+                            block = acc[down, :, up * width : (up + 1) * width]
+                            across, along = pl.ds(b * width, width), pl.ds(a * width, width)
+                            whole[across, along] = block.astype(jnp.bfloat16)
                             if a != b:
-                                whole[b * width : (b + 1) * width, a * width : (a + 1) * width] = (
-                                    block.T.astype(jnp.bfloat16)
-                                )
-
-        pl.semaphore_wait(barrier, slabs - 1)
+                                whole[along, across] = block.T.astype(jnp.bfloat16)
+
+        pl.semaphore_wait(barrier, slabs - 1 + bands - 1)
         copies = []
         for d in range(1, slabs):
             peer = lax.rem(me + d, slabs)
@@ -354,8 +355,29 @@
         for d, copy in enumerate(copies):
             copy.wait_recv()
             total = total + landed[d].astype(jnp.float32)
-        out_ref[...] = total.astype(jnp.bfloat16)
-        for copy in copies:
+        for q in range(bands):
+            mine[q] = total[:, q * width : (q + 1) * width].astype(jnp.bfloat16)
+        across = []
+        for d in range(1, bands):
+            peer = lax.rem(band + d, bands)
+            across.append(
+                pltpu.make_async_remote_copy(
+                    src_ref=mine.at[peer],
+                    dst_ref=got.at[d - 1],
+                    send_sem=band_send.at[d - 1],
+                    recv_sem=band_recv.at[d - 1],
+                    device_id={"band": peer},
+                    device_id_type=pl.DeviceIdType.MESH,
+                )
+            )
+        for copy in across:
+            copy.start()
+        total = mine[band].astype(jnp.float32)
+        for d, copy in enumerate(across):
+            copy.wait_recv()
+            total = total + got[d].astype(jnp.float32)
+        out_ref[...] = total.T / nodes_all
+        for copy in copies + across:
             copy.wait_send()
 
 
@@ -384,26 +406,32 @@
     states = bands * columns
     share = states // slabs
     dma = pltpu.SemaphoreType.DMA
-    sums = pl.pallas_call(
-        functools.partial(combine_kernel, slabs, bands, ups, downs),
+    narrow = jnp.bfloat16
+    projected = pl.pallas_call(
+        functools.partial(
+            combine_kernel, slabs, bands, ups, downs, FACE * ((EDGE - 1) * slabs + 1)
+        ),
         grid=(EDGE,),
         in_specs=[pl.BlockSpec((nodes // EDGE, columns), lambda z: (z, 0))] * (ups + downs),
-        out_specs=pl.BlockSpec((share, states), lambda z: (0, 0)),
-        out_shape=jax.ShapeDtypeStruct((share, states), jnp.bfloat16),
+        out_specs=pl.BlockSpec((columns, share), lambda z: (0, 0)),
+        out_shape=jax.ShapeDtypeStruct((columns, share), jnp.float32),
         scratch_shapes=[
-            pltpu.VMEM((ups, downs, columns, columns), jnp.float32),
-            pltpu.VMEM((states, states), jnp.bfloat16),
-            pltpu.VMEM((slabs - 1, share, states), jnp.bfloat16),
+            pltpu.VMEM((downs, columns, ups * columns), jnp.float32),
+            pltpu.VMEM((states, states), narrow),
+            pltpu.VMEM((slabs - 1, share, states), narrow),
+            pltpu.VMEM((bands, share, columns), narrow),
+            pltpu.VMEM((bands - 1, share, columns), narrow),
             dma((slabs - 1,)),
             dma((slabs - 1,)),
+            dma((bands - 1,)),
+            dma((bands - 1,)),
         ],
         compiler_params=pltpu.CompilerParams(
             collective_id=2, has_side_effects=True, vmem_limit_bytes=VMEM_BYTES
         ),
         name="combine",
     )(*rows, *images)
-    totals = lax.psum_scatter(sums, "band", scatter_dimension=1, tiled=True).astype(jnp.float32)
-    return out, totals.T / (FACE * ((EDGE - 1) * slabs + 1))
+    return out, projected
 
 
 def solution(mesh):

time: 314 us -> 282 us (0.90)
  waiting for transfers between devices: 71.2 us -> 40.4 us
  between operations: 15.5 us -> 2.16 us
  Pallas kernels: 204 us -> 215 us
    reduce_scatter x1 -> x0, waiting for transfers between devices: 30.8 us -> none  [project(): lax.psum_scatter(sums, 'band', scatter_dimension=1, tiled=True)]
    pallas_call x1, Pallas kernels: 92.9 us -> 104 us  [project(): pl.pallas_call(functools.partial(combine_kernel, slabs, bands, ups, downs...]
  transfers between devices with their start and end apart: 4 -> 3, of which waited for: 2 -> 1; matrix products, arithmetic and copies ran while one was open for 0% -> 0% of each run, Pallas kernels for 5% -> 5%
where the time goes in v3:
time: 282 us; the launch traced here: 280 us
  Pallas kernels  215 us (76%)
  waiting for transfers between devices  40.4 us (14%)
  starting transfers between devices  11.9 us (4%)
  local copies, waits for them, and re-layouts  7.67 us (3%)
    pallas_call x1, Pallas kernels, project(): pl.pallas_call(functools.partial(combine_kernel, slabs, bands, ups, downs...  104 us
    pallas_call x1, Pallas kernels, local(): pl.pallas_call(functools.partial(filter_kernel, slabs), in_specs=[smem(),...  71.4 us
    ppermute x3, waiting for transfers between devices, move(): return lax.ppermute(array, ('space', 'band'), perm)  40.4 us
    pallas_call x1, Pallas kernels, local(): pl.pallas_call(sort_kernel, grid=(EDGE,), in_specs=[whole(FACE, EDGE), pl...  24.8 us
    pallas_call x1, Pallas kernels, local(): unsort(order, filtered)  14.9 us
    ppermute x3, starting transfers between devices, move(): return lax.ppermute(array, ('space', 'band'), perm)  11.9 us
  transfers between devices with their start and end apart: 3, of which 1 were waited for; matrix products, arithmetic and copies ran while one was open for 0% of the time, Pallas kernels for 5%

profile of v3, /device:TPU:0, one launch (start us, length us, event | category | flops | bytes accessed | tf_op | source)
XLA Modules:
  0.0 280.2 jit_solution(14514189333787360309)
XLA Ops:
  0.6 0.0 copy-start
  0.6 0.0 copy-start.2
  2.0 1.3 reshape.46
  3.3 0.8 slice_reduce_fusion
  4.2 0.1 slice_bitcast_fusion
  4.3 1.4 copy.33
  5.7 0.1 pad_add_fusion
  5.8 0.1 slice_add_fusion
  5.9 0.0 copy-done.2
  5.9 0.7 reshape.50.potential_ref
  6.6 0.1 copy.35
  6.7 0.4 copy.34
  7.2 0.1 reshape.49
  7.3 0.1 fusion.12
  7.4 1.1 copy.37.order_ref
  8.5 0.6 pad_maximum_fusion.bounds_ref
  9.1 0.0 copy-done
  9.1 1.6 convolution_convert_fusion.matrix_ref
  10.7 24.8 %sort_rows.1 = (f32[2,10368,128]{2,1,0:T(8,128)}, f32[10368,128]{1,0:T(8,128)}) custom-call(s32[1296,8]{1,0:T(8,128)} %copy.37.order_ref, bf16[10368,256]{1,0:T(8,128)(2,1)} %states_ref.1, f32[8,1296]{1,0:T(8,128)} %reshape.50.potential_ref), custom_call_target="tpu_custom_call" | custom-call | tf_op jit(solution)/shard_map/sort_rows/pallas_call | solution.py:219
  35.6 71.4 %filter_states.1 = (bf16[10368,256]{1,0:T(8,128)(2,1)}, bf16[10368,256]{1,0:T(8,128)(2,1)}) custom-call(f32[2]{0:T(128)} %pad_maximum_fusion.bounds_ref, f32[25]{0:T(128)} %scale_ref.1, f32[2,10368,128]{2,1,0:T(8,128)} %get-tuple-element.9.u_hbm, f32[10368,128]{1,0:T(8,128)} %get-tuple-element.10.pot_ref, bf16[512,512]{1,0:T(8,128)(2,1)} %convolution_convert_fusion.matrix_ref), custom_call_target="tpu_custom_call" | custom-call | tf_op jit(solution)/shard_map/filter_states/pallas_call | solution.py:240
  107.0 5.8 %collective-permute-start = (bf16[10368,256]{1,0:T(8,128)(2,1)}, bf16[10368,256]{1,0:T(8,128)(2,1)}, u32[]{:S(2)}, u32[]{:S(2)}) collective-permute-start(bf16[10368,256]{1,0:T(8,128)(2,1)} %get-tuple-element.11.f_ref.refs_0_), channel_id=1, source_target_pairs={{0,1},{1,2},{7,6},{6,5},{8,9},{9,10},{15,14},{14,13},{16,17},{17,1... | collective-permute-start | bytes 15925256 | tf_op jit(solution)/shard_map/ppermute | solution.py:395
  112.8 0.7 broadcast_subtract_fusion.order_ref
  113.5 0.0 copy-start.1
  113.5 14.9 %unsort_rows.1 = bf16[10368,256]{1,0:T(8,128)(2,1)} custom-call(s32[8,1296]{1,0:T(8,128)} %broadcast_subtract_fusion.order_ref, bf16[10368,256]{1,0:T(8,128)(2,1)} %get-tuple-element.11.f_ref.refs_0_), custom_call_target="tpu_custom_call" | custom-call | flops 6879707136 | bytes 10616832 | tf_op jit(solution)/shard_map/unsort_rows/pallas_call | solution.py:268
  128.4 40.4 %collective-permute-done.refs_1_ = bf16[10368,256]{1,0:T(8,128)(2,1)} collective-permute-done((bf16[10368,256]{1,0:T(8,128)(2,1)}, bf16[10368,256]{1,0:T(8,128)(2,1)}, u32[]{:S(2)}, u32[]{:S(2)}) %collective-permute-start) | collective-permute-done | bytes 5308448 | tf_op jit(solution)/shard_map/ppermute | solution.py:395
  168.7 3.0 %collective-permute-start.1 = (bf16[10368,256]{1,0:T(8,128)(2,1)}, bf16[10368,256]{1,0:T(8,128)(2,1)}, u32[]{:S(2)}, u32[]{:S(2)}) collective-permute-start(bf16[10368,256]{1,0:T(8,128)(2,1)} %collective-permute-done.refs_1_), channel_id=1, source_target_pairs={{1,2},{6,5},{9,10},{14,13},{17,18},{22,21},{25,26},{30,29}} | collective-permute-start | bytes 15925256 | tf_op jit(solution)/shard_map/ppermute | solution.py:395
  171.8 0.0 copy-done.1
  171.8 3.0 %collective-permute-start.2 = (bf16[10368,256]{1,0:T(8,128)(2,1)S(1)}, bf16[10368,256]{1,0:T(8,128)(2,1)}, u32[]{:S(2)}, u32[]{:S(2)}) collective-permute-start(bf16[10368,256]{1,0:T(8,128)(2,1)S(1)} %copy-done.1), channel_id=1, source_target_pairs={{3,2},{4,5},{11,10},{12,13},{19,18},{20,21},{27,26},{28,29}} | collective-permute-start | bytes 15925256 | tf_op jit(solution)/shard_map/ppermute | solution.py:395
  174.8 0.0 collective-permute-done.1.refs_2_
  174.8 0.0 collective-permute-done.2.refs_4_
  174.8 103.8 %combine.1 = f32[256,128]{1,0:T(8,128)} custom-call(bf16[10368,256]{1,0:T(8,128)(2,1)} %get-tuple-element.11.f_ref.refs_0_, bf16[10368,256]{1,0:T(8,128)(2,1)} %collective-permute-done.refs_1_, bf16[10368,256]{1,0:T(8,128)(2,1)} %collective-permute-done.1.refs_2_, bf16[10368,256]{1,0:T(8,128)(2,1)} %get-tuple-element.15.refs_3_, ...), custom_call_target="tpu_custom_call" | custom-call | tf_op jit(solution)/shard_map/combine/pallas_call | solution.py:410
  278.6 1.6 copy.41
  (4 shorter events, 0.1 us)
Async XLA Ops:
  0.6 8.5 %copy-start = (bf16[512,512]{1,0:T(8,128)(2,1)S(1)}, bf16[512,512]{1,0:T(8,128)(2,1)}, u32[]{:S(2)}) copy-start(bf16[512,512]{1,0:T(8,128)(2,1)} %param.9) | copy-start | bytes 1572868
  0.6 5.2 %copy-start.2 = (f32[10368]{0:T(1024)S(1)}, f32[10368]{0:T(1024)}, u32[]{:S(2)}) copy-start(f32[10368]{0:T(1024)} %param.8) | copy-start | bytes 124420
  107.0 61.7 %collective-permute-start = (bf16[10368,256]{1,0:T(8,128)(2,1)}, bf16[10368,256]{1,0:T(8,128)(2,1)}, u32[]{:S(2)}, u32[]{:S(2)}) collective-permute-start(bf16[10368,256]{1,0:T(8,128)(2,1)} %get-tuple-element.11.f_ref.refs_0_), channel_id=1, source_target_pairs={{0,1},{1,2},{7,6},{6,5},{8,9},{9,10},{15,14},{14,13},{16,17},{17,1... | collective-permute-start | bytes 15925256 | tf_op jit(solution)/shard_map/ppermute | solution.py:395
  113.5 58.3 %copy-start.1 = (bf16[10368,256]{1,0:T(8,128)(2,1)S(1)}, bf16[10368,256]{1,0:T(8,128)(2,1)}, u32[]{:S(2)}) copy-start(bf16[10368,256]{1,0:T(8,128)(2,1)} %get-tuple-element.15.refs_3_) | copy-start | bytes 15925252
  168.7 6.1 %collective-permute-start.1 = (bf16[10368,256]{1,0:T(8,128)(2,1)}, bf16[10368,256]{1,0:T(8,128)(2,1)}, u32[]{:S(2)}, u32[]{:S(2)}) collective-permute-start(bf16[10368,256]{1,0:T(8,128)(2,1)} %collective-permute-done.refs_1_), channel_id=1, source_target_pairs={{1,2},{6,5},{9,10},{14,13},{17,18},{22,21},{25,26},{30,29}} | collective-permute-start | bytes 15925256 | tf_op jit(solution)/shard_map/ppermute | solution.py:395
  171.8 3.0 %collective-permute-start.2 = (bf16[10368,256]{1,0:T(8,128)(2,1)S(1)}, bf16[10368,256]{1,0:T(8,128)(2,1)}, u32[]{:S(2)}, u32[]{:S(2)}) collective-permute-start(bf16[10368,256]{1,0:T(8,128)(2,1)S(1)} %copy-done.1), channel_id=1, source_target_pairs={{3,2},{4,5},{11,10},{12,13},{19,18},{20,21},{27,26},{28,29}} | collective-permute-start | bytes 15925256 | tf_op jit(solution)/shard_map/ppermute | solution.py:395

commit v4 on v3

--- a/solution.py
+++ b/solution.py
@@ -59,8 +59,8 @@
 
 
 def filter_kernel(
-    count, bounds_ref, scale_ref, u_hbm, pot_ref, matrix_ref, f_ref, w_ref,
-    even, odd, acc, send, recv, load_sem, send_sem, recv_sem,
+    count, bands, bounds_ref, scale_ref, u_hbm, pot_ref, matrix_ref, f_ref, w_ref, next_hbm,
+    even, odd, acc, send, recv, load_sem, send_sem, recv_sem, hop_send, hop_recv,
 ):
     halves = acc.shape[0]
     nodes = acc.shape[1]
@@ -69,18 +69,31 @@
     has_up = me < count - 1
     barrier = pltpu.get_barrier_semaphore()
 
-    def greet(there, other):
+    band = lax.axis_index("band")
+    swap = lax.rem(me, 2) == 1
+    role = jnp.where(swap, bands - 1 - band, band)
+    onward = jnp.where(swap, -1, 1)
+    gives = role < bands // 2
+    takes = (role > 0) & (role <= bands // 2)
+
+    def greet(there, axis, other):
         @pl.when(there)
         def _():
             pl.semaphore_signal(
-                barrier, inc=1, device_id={"space": other}, device_id_type=pl.DeviceIdType.MESH
+                barrier, inc=1, device_id={axis: other}, device_id_type=pl.DeviceIdType.MESH
             )
 
     load = pltpu.make_async_copy(u_hbm, even, load_sem)
     load.start()
-    greet(has_low, me - 1)
-    greet(has_up, me + 1)
-    pl.semaphore_wait(barrier, jnp.where(has_low, 1, 0) + jnp.where(has_up, 1, 0))
+    peers = (
+        (has_low, "space", me - 1),
+        (has_up, "space", me + 1),
+        (gives, "band", band + onward),
+        (takes, "band", band - onward),
+    )
+    for peer in peers:
+        greet(*peer)
+    pl.semaphore_wait(barrier, sum(jnp.where(peer[0], 1, 0) for peer in peers))
     load.wait()
 
     center = bounds_ref[0]
@@ -99,6 +112,17 @@
             send_sem=send_sem.at[step % 2, h, side],
             recv_sem=recv_sem.at[step % 2, h, 1 - side],
             device_id={"space": me - 1 if side == 0 else me + 1},
+            device_id_type=pl.DeviceIdType.MESH,
+        )
+
+    def hop(h):
+        part = pl.ds(h * LANES, LANES)
+        return pltpu.make_async_remote_copy(
+            src_ref=f_ref.at[:, part],
+            dst_ref=next_hbm.at[:, part],
+            send_sem=hop_send.at[h],
+            recv_sem=hop_recv.at[h],
+            device_id={"band": band + onward},
             device_id_type=pl.DeviceIdType.MESH,
         )
 
@@ -172,6 +196,10 @@
         lax.fori_loop(0, SIDE, body, 0)
         if step == STEPS - 1:
             f_ref[:, h * LANES : (h + 1) * LANES] = fresh[h].astype(jnp.bfloat16)
+
+            @pl.when(gives)
+            def _():
+                hop(h).start()
 
     fields = (even, odd)
     for h in range(halves):
@@ -188,6 +216,14 @@
                 ship(step + 1, h)
             else:
                 w_ref[:, h * LANES : (h + 1) * LANES] = acc[h].astype(jnp.bfloat16)
+    for h in range(halves):
+        @pl.when(gives)
+        def _(h=h):
+            hop(h).wait_send()
+
+        @pl.when(takes)
+        def _(h=h):
+            hop(h).wait_recv()
 
 
 def vmem():
@@ -237,14 +273,14 @@
     field = pltpu.VMEM((halves, nodes, LANES), jnp.float32)
     faces = pltpu.VMEM((2, halves, 2, FACE, LANES), jnp.bfloat16)
     narrow = jax.ShapeDtypeStruct((nodes, columns), jnp.bfloat16)
-    filtered, image = pl.pallas_call(
-        functools.partial(filter_kernel, slabs),
+    filtered, image, landed = pl.pallas_call(
+        functools.partial(filter_kernel, slabs, bands),
         in_specs=[smem(), smem(), pl.BlockSpec(memory_space=pl.ANY), vmem(), vmem()],
-        out_specs=[vmem(), vmem()],
-        out_shape=[narrow, narrow],
+        out_specs=[vmem(), vmem(), pl.BlockSpec(memory_space=pl.ANY)],
+        out_shape=[narrow, narrow, narrow],
         scratch_shapes=[
             field, field, field, faces, faces,
-            dma, dma((2, halves, 2)), dma((2, halves, 2)),
+            dma, dma((2, halves, 2)), dma((2, halves, 2)), dma((halves,)), dma((halves,)),
         ],
         compiler_params=pltpu.CompilerParams(
             collective_id=1, has_side_effects=True, vmem_limit_bytes=VMEM_BYTES
@@ -265,7 +301,7 @@
         ),
         name="unsort_rows",
     )
-    return project(filtered, image, slabs, bands, lambda: unsort(order, filtered))
+    return unsort(order, filtered), project(filtered, landed, image, slabs, bands)
 
 
 def held_by(up, down, bands):
@@ -275,9 +311,20 @@
     return first, last
 
 
+def early_kernel(f_ref, next_ref, w_ref, out_ref):
+    @pl.when(pl.program_id(0) == 0)
+    def _():
+        out_ref[...] = jnp.zeros_like(out_ref)
+
+    side = jnp.concatenate([f_ref[...], next_ref[...]], axis=1)
+    out_ref[...] += lax.dot_general(
+        w_ref[...], side, (((0,), (0,)), ((), ())), preferred_element_type=jnp.float32
+    )
+
+
 def combine_kernel(slabs, bands, ups, downs, nodes_all, *refs):
-    f_refs, w_refs = refs[:ups], refs[ups : ups + downs]
-    out_ref, acc, whole, landed, mine, got, send_sem, recv_sem, band_send, band_recv = refs[ups + downs :]
+    f_refs, w_refs, early_ref = refs[:ups], refs[ups : ups + downs], refs[ups + downs]
+    out_ref, acc, whole, landed, mine, got, send_sem, recv_sem, band_send, band_recv = refs[ups + downs + 1 :]
     step = pl.program_id(0)
     width = acc.shape[1]
     rows = whole.shape[0] // slabs
@@ -298,6 +345,7 @@
                     device_id_type=pl.DeviceIdType.MESH,
                 )
         acc[...] = jnp.zeros_like(acc)
+        acc[0, :, : 2 * width] = early_ref[...]
 
     held = {}
     for r in range(bands):
@@ -311,9 +359,13 @@
         @pl.when(role == r)
         def _(images=images):
             for down, fields in images.items():
+                begin = 0 if down else 2
+                fields = fields[begin:]
+                if not fields:
+                    continue
                 sides = [f_refs[up][...] for up in fields]
                 side = sides[0] if len(sides) == 1 else jnp.concatenate(sides, axis=1)
-                acc[down, :, : len(fields) * width] += lax.dot_general(
+                acc[down, :, begin * width : (begin + len(fields)) * width] += lax.dot_general(
                     w_refs[down][...], side, (((0,), (0,)), ((), ())), preferred_element_type=jnp.float32
                 )
 
@@ -381,7 +433,7 @@
             copy.wait_send()
 
 
-def project(filtered, image, slabs, bands, unsort):
+def project(filtered, landed, image, slabs, bands):
     nodes, columns = filtered.shape
     middle = bands // 2
 
@@ -394,8 +446,7 @@
                 perm.append((s * bands + a, s * bands + b))
         return lax.ppermute(array, ("space", "band"), perm)
 
-    rows = [filtered, move(filtered, [(a, a + 1) for a in range(middle)])]
-    out, rows[-1], image = lax.optimization_barrier((unsort(), rows[-1], image))
+    rows = [filtered, landed]
     for hop in range(2, middle + 1):
         rows.append(move(rows[-1], [(a, a + 1) for a in range(hop - 1, middle)]))
     images = [image]
@@ -407,12 +458,26 @@
     share = states // slabs
     dma = pltpu.SemaphoreType.DMA
     narrow = jnp.bfloat16
+    chunk = pl.BlockSpec((nodes // EDGE, columns), lambda z: (z, 0))
+    early = pl.pallas_call(
+        early_kernel,
+        grid=(EDGE,),
+        in_specs=[chunk] * 3,
+        out_specs=pl.BlockSpec((columns, 2 * columns), lambda z: (0, 0)),
+        out_shape=jax.ShapeDtypeStruct((columns, 2 * columns), jnp.float32),
+        compiler_params=pltpu.CompilerParams(vmem_limit_bytes=VMEM_BYTES),
+        cost_estimate=pl.CostEstimate(
+            flops=4 * nodes * columns * columns, bytes_accessed=6 * nodes * columns, transcendentals=0
+        ),
+        name="early_products",
+    )(filtered, landed, image)
     projected = pl.pallas_call(
         functools.partial(
             combine_kernel, slabs, bands, ups, downs, FACE * ((EDGE - 1) * slabs + 1)
         ),
         grid=(EDGE,),
-        in_specs=[pl.BlockSpec((nodes // EDGE, columns), lambda z: (z, 0))] * (ups + downs),
+        in_specs=[chunk] * (ups + downs)
+        + [pl.BlockSpec((columns, 2 * columns), lambda z: (0, 0))],
         out_specs=pl.BlockSpec((columns, share), lambda z: (0, 0)),
         out_shape=jax.ShapeDtypeStruct((columns, share), jnp.float32),
         scratch_shapes=[
@@ -430,8 +495,8 @@
             collective_id=2, has_side_effects=True, vmem_limit_bytes=VMEM_BYTES
         ),
         name="combine",
-    )(*rows, *images)
-    return out, projected
+    )(*rows, *images, early)
+    return projected
 
 
 def solution(mesh):

time: 282 us -> 271 us (0.961)
  waiting for transfers between devices: 40.4 us -> 0.01 us
  Pallas kernels: 215 us -> 249 us
  starting transfers between devices: 11.9 us -> 4.03 us
    pallas_call x1 -> x2, Pallas kernels: 71.4 us -> 130 us  [the longest x1 120 us: local(): pl.pallas_call(functools.partial(filter_kernel, slabs, bands), in_specs=[...]
    ppermute x3 -> x2, waiting for transfers between devices: 40.4 us -> 0.01 us  [move(): return lax.ppermute(array, ('space', 'band'), perm)]
    pallas_call x1, Pallas kernels: 104 us -> 79.7 us  [project(): pl.pallas_call(functools.partial(combine_kernel, slabs, bands, ups, downs...]
    ppermute x3 -> x2, starting transfers between devices: 11.9 us -> 4.03 us  [move(): return lax.ppermute(array, ('space', 'band'), perm)]
  transfers between devices with their start and end apart: 3 -> 2, of which waited for: 1 -> 0; matrix products, arithmetic and copies ran while one was open for 0% -> 0% of each run, Pallas kernels for 5% -> 9%
where the time goes in v4:
time: 271 us; the launch traced here: 268 us
  Pallas kernels  249 us (92%)
  local copies, waits for them, and re-layouts  10 us (4%)
  starting transfers between devices  4.03 us (1%)
    pallas_call x1, Pallas kernels, local(): pl.pallas_call(functools.partial(filter_kernel, slabs, bands), in_specs=[...  120 us
    pallas_call x1, Pallas kernels, project(): pl.pallas_call(functools.partial(combine_kernel, slabs, bands, ups, downs...  79.7 us
    pallas_call x1, Pallas kernels, local(): pl.pallas_call(sort_kernel, grid=(EDGE,), in_specs=[whole(FACE, EDGE), pl...  24.8 us
    pallas_call x1, Pallas kernels, local(): unsort(order, filtered)  14.7 us
    pallas_call x1, Pallas kernels, project(): pl.pallas_call(early_kernel, grid=(EDGE,), in_specs=[chunk] * 3, out_spec...  10.3 us
  transfers between devices with their start and end apart: 2, of which 0 were waited for; matrix products, arithmetic and copies ran while one was open for 0% of the time, Pallas kernels for 9%

profile of v4, /device:TPU:0, one launch (start us, length us, event | category | flops | bytes accessed | tf_op | source)
XLA Modules:
  0.0 268.4 jit_solution(8447876752480827021)
XLA Ops:
  0.6 0.0 copy-start
  0.6 0.0 copy-start.2
  0.7 1.4 reshape.46
  2.0 0.1 slice_bitcast_fusion
  2.1 0.8 slice_reduce_fusion
  2.9 1.4 copy.33
  4.4 0.1 slice_add_fusion
  4.4 0.1 pad_add_fusion
  5.9 0.4 copy.34
  6.3 0.1 copy.35
  6.5 0.1 reshape.49
  6.6 0.1 fusion.12
  6.6 1.1 copy.37.order_ref
  7.7 0.0 copy-done.2
  7.7 0.7 reshape.50.potential_ref
  8.5 0.7 pad_maximum_fusion.bounds_ref
  9.2 0.0 copy-done
  9.2 1.6 convolution_convert_fusion.matrix_ref
  10.8 24.8 %sort_rows.1 = (f32[2,10368,128]{2,1,0:T(8,128)}, f32[10368,128]{1,0:T(8,128)}) custom-call(s32[1296,8]{1,0:T(8,128)} %copy.37.order_ref, bf16[10368,256]{1,0:T(8,128)(2,1)} %states_ref.1, f32[8,1296]{1,0:T(8,128)} %reshape.50.potential_ref), custom_call_target="tpu_custom_call" | custom-call | tf_op jit(solution)/shard_map/sort_rows/pallas_call | solution.py:255
  35.6 119.5 %filter_states.1 = (bf16[10368,256]{1,0:T(8,128)(2,1)}, bf16[10368,256]{1,0:T(8,128)(2,1)}, bf16[10368,256]{1,0:T(8,128)(2,1)}) custom-call(f32[2]{0:T(128)} %pad_maximum_fusion.bounds_ref, f32[25]{0:T(128)} %scale_ref.1, f32[2,10368,128]{2,1,0:T(8,128)} %get-tuple-element.7.u_hbm, f32[10368,128]{1,0:T(8,128)} %get-tuple-element.8.pot_ref, ...), custom_call_target="tpu_custom_call" | custom-call | tf_op jit(solution)/shard_map/filter_states/pallas_call | solution.py:276
  155.2 1.0 collective-permute-start
  156.2 3.0 %collective-permute-start.1 = (bf16[10368,256]{1,0:T(8,128)(2,1)}, bf16[10368,256]{1,0:T(8,128)(2,1)}, u32[]{:S(2)}, u32[]{:S(2)}) collective-permute-start(bf16[10368,256]{1,0:T(8,128)(2,1)} %get-tuple-element.11.w_ref.refs_3_), channel_id=1, source_target_pairs={{3,2},{4,5},{11,10},{12,13},{19,18},{20,21},{27,26},{28,29}} | collective-permute-start | bytes 15925256 | tf_op jit(solution)/shard_map/ppermute | solution.py:447
  159.2 10.3 %early_products.1.refs_5_ = f32[256,512]{1,0:T(8,128)} custom-call(bf16[10368,256]{1,0:T(8,128)(2,1)} %get-tuple-element.9.f_ref.refs_0_, bf16[10368,256]{1,0:T(8,128)(2,1)} %get-tuple-element.10.next_ref.refs_1_, bf16[10368,256]{1,0:T(8,128)(2,1)} %get-tuple-element.11.w_ref.refs_3_), custom_call_target="tpu_custom_call" | custom-call | flops 2717908992 | bytes 15925248 | tf_op jit(solution)/shard_map/early_products/pallas_call | solution.py:462
  169.5 0.7 broadcast_subtract_fusion.order_ref
  170.2 14.7 %unsort_rows.1 = bf16[10368,256]{1,0:T(8,128)(2,1)} custom-call(s32[8,1296]{1,0:T(8,128)} %broadcast_subtract_fusion.order_ref, bf16[10368,256]{1,0:T(8,128)(2,1)} %get-tuple-element.9.f_ref.refs_0_), custom_call_target="tpu_custom_call" | custom-call | flops 6879707136 | bytes 10616832 | tf_op jit(solution)/shard_map/unsort_rows/pallas_call | solution.py:304
  184.9 0.0 collective-permute-done.refs_2_
  184.9 0.0 copy-start.1
  184.9 0.0 collective-permute-done.1.refs_4_
  184.9 2.3 copy-done.1
  187.2 79.7 %combine.1 = f32[256,128]{1,0:T(8,128)} custom-call(bf16[10368,256]{1,0:T(8,128)(2,1)} %get-tuple-element.9.f_ref.refs_0_, bf16[10368,256]{1,0:T(8,128)(2,1)} %get-tuple-element.10.next_ref.refs_1_, bf16[10368,256]{1,0:T(8,128)(2,1)} %copy-done.1, bf16[10368,256]{1,0:T(8,128)(2,1)} %get-tuple-element.11.w_ref.refs_3_, ...), custom_call_target="tpu_custom_call" | custom-call | tf_op jit(solution)/shard_map/combine/pallas_call | solution.py:474
  266.9 1.6 copy.41
  (4 shorter events, 0.1 us)
Async XLA Ops:
  0.6 8.5 %copy-start = (bf16[512,512]{1,0:T(8,128)(2,1)S(1)}, bf16[512,512]{1,0:T(8,128)(2,1)}, u32[]{:S(2)}) copy-start(bf16[512,512]{1,0:T(8,128)(2,1)} %param.9) | copy-start | bytes 1572868
  0.6 7.1 %copy-start.2 = (f32[10368]{0:T(1024)S(1)}, f32[10368]{0:T(1024)}, u32[]{:S(2)}) copy-start(f32[10368]{0:T(1024)} %param.8) | copy-start | bytes 124420
  155.2 29.7 %collective-permute-start = (bf16[10368,256]{1,0:T(8,128)(2,1)}, bf16[10368,256]{1,0:T(8,128)(2,1)S(1)}, u32[]{:S(2)}, u32[]{:S(2)}) collective-permute-start(bf16[10368,256]{1,0:T(8,128)(2,1)} %get-tuple-element.10.next_ref.refs_1_), channel_id=1, source_target_pairs={{1,2},{6,5},{9,10},{14,13},{17,18},{22,21},{25,26},{30,29}} | collective-permute-start | bytes 15925256 | tf_op jit(solution)/shard_map/ppermute | solution.py:447
  156.2 28.7 %collective-permute-start.1 = (bf16[10368,256]{1,0:T(8,128)(2,1)}, bf16[10368,256]{1,0:T(8,128)(2,1)}, u32[]{:S(2)}, u32[]{:S(2)}) collective-permute-start(bf16[10368,256]{1,0:T(8,128)(2,1)} %get-tuple-element.11.w_ref.refs_3_), channel_id=1, source_target_pairs={{3,2},{4,5},{11,10},{12,13},{19,18},{20,21},{27,26},{28,29}} | collective-permute-start | bytes 15925256 | tf_op jit(solution)/shard_map/ppermute | solution.py:447
  184.9 2.3 copy-start.1

commit v5 on v4

--- a/solution.py
+++ b/solution.py
@@ -159,7 +159,7 @@
             cells(u, h, (4 * i + 2, 4 * i + 3))
             return carry
 
-        lax.fori_loop(0, CELLS // 4, body, 0)
+        lax.fori_loop(0, CELLS // 4, body, 0, unroll=2)
         cells(u, h, (CELLS - 1,))
 
     def ship(step, h):

time: 271 us -> 270 us (level)
  no operation moved by 1% of the time
where the time goes in v5:
time: 270 us; the launch traced here: 268 us
  Pallas kernels  248 us (92%)
  local copies, waits for them, and re-layouts  10 us (4%)
  starting transfers between devices  4.03 us (1%)
    pallas_call x1, Pallas kernels, local(): pl.pallas_call(functools.partial(filter_kernel, slabs, bands), in_specs=[...  119 us
    pallas_call x1, Pallas kernels, project(): pl.pallas_call(functools.partial(combine_kernel, slabs, bands, ups, downs...  80 us
    pallas_call x1, Pallas kernels, local(): pl.pallas_call(sort_kernel, grid=(EDGE,), in_specs=[whole(FACE, EDGE), pl...  24.8 us
    pallas_call x1, Pallas kernels, local(): unsort(order, filtered)  14.7 us
    pallas_call x1, Pallas kernels, project(): pl.pallas_call(early_kernel, grid=(EDGE,), in_specs=[chunk] * 3, out_spec...  10.3 us
  transfers between devices with their start and end apart: 2, of which 0 were waited for; matrix products, arithmetic and copies ran while one was open for 0% of the time, Pallas kernels for 9%

profile of v5, /device:TPU:0, one launch (start us, length us, event | category | flops | bytes accessed | tf_op | source)
XLA Modules:
  0.0 267.9 jit_solution(13427583100405066125)
XLA Ops:
  0.6 0.0 copy-start
  0.6 0.0 copy-start.2
  0.7 1.4 reshape.46
  2.0 0.1 slice_bitcast_fusion
  2.1 0.8 slice_reduce_fusion
  2.9 1.4 copy.33
  4.4 0.1 slice_add_fusion
  4.4 0.1 pad_add_fusion
  5.9 0.4 copy.34
  6.3 0.1 copy.35
  6.5 0.1 reshape.49
  6.6 0.1 fusion.12
  6.6 1.1 copy.37.order_ref
  7.7 0.0 copy-done.2
  7.7 0.7 reshape.50.potential_ref
  8.5 0.7 pad_maximum_fusion.bounds_ref
  9.2 0.0 copy-done
  9.2 1.6 convolution_convert_fusion.matrix_ref
  10.8 24.8 %sort_rows.1 = (f32[2,10368,128]{2,1,0:T(8,128)}, f32[10368,128]{1,0:T(8,128)}) custom-call(s32[1296,8]{1,0:T(8,128)} %copy.37.order_ref, bf16[10368,256]{1,0:T(8,128)(2,1)} %states_ref.1, f32[8,1296]{1,0:T(8,128)} %reshape.50.potential_ref), custom_call_target="tpu_custom_call" | custom-call | tf_op jit(solution)/shard_map/sort_rows/pallas_call | solution.py:255
  35.6 118.6 %filter_states.1 = (bf16[10368,256]{1,0:T(8,128)(2,1)}, bf16[10368,256]{1,0:T(8,128)(2,1)}, bf16[10368,256]{1,0:T(8,128)(2,1)}) custom-call(f32[2]{0:T(128)} %pad_maximum_fusion.bounds_ref, f32[25]{0:T(128)} %scale_ref.1, f32[2,10368,128]{2,1,0:T(8,128)} %get-tuple-element.7.u_hbm, f32[10368,128]{1,0:T(8,128)} %get-tuple-element.8.pot_ref, ...), custom_call_target="tpu_custom_call" | custom-call | tf_op jit(solution)/shard_map/filter_states/pallas_call | solution.py:276
  154.3 1.0 collective-permute-start
  155.3 3.0 %collective-permute-start.1 = (bf16[10368,256]{1,0:T(8,128)(2,1)}, bf16[10368,256]{1,0:T(8,128)(2,1)}, u32[]{:S(2)}, u32[]{:S(2)}) collective-permute-start(bf16[10368,256]{1,0:T(8,128)(2,1)} %get-tuple-element.11.w_ref.refs_3_), channel_id=1, source_target_pairs={{3,2},{4,5},{11,10},{12,13},{19,18},{20,21},{27,26},{28,29}} | collective-permute-start | bytes 15925256 | tf_op jit(solution)/shard_map/ppermute | solution.py:447
  158.3 10.3 %early_products.1.refs_5_ = f32[256,512]{1,0:T(8,128)} custom-call(bf16[10368,256]{1,0:T(8,128)(2,1)} %get-tuple-element.9.f_ref.refs_0_, bf16[10368,256]{1,0:T(8,128)(2,1)} %get-tuple-element.10.next_ref.refs_1_, bf16[10368,256]{1,0:T(8,128)(2,1)} %get-tuple-element.11.w_ref.refs_3_), custom_call_target="tpu_custom_call" | custom-call | flops 2717908992 | bytes 15925248 | tf_op jit(solution)/shard_map/early_products/pallas_call | solution.py:462
  168.6 0.7 broadcast_subtract_fusion.order_ref
  169.3 14.7 %unsort_rows.1 = bf16[10368,256]{1,0:T(8,128)(2,1)} custom-call(s32[8,1296]{1,0:T(8,128)} %broadcast_subtract_fusion.order_ref, bf16[10368,256]{1,0:T(8,128)(2,1)} %get-tuple-element.9.f_ref.refs_0_), custom_call_target="tpu_custom_call" | custom-call | flops 6879707136 | bytes 10616832 | tf_op jit(solution)/shard_map/unsort_rows/pallas_call | solution.py:304
  184.0 0.0 collective-permute-done.refs_2_
  184.0 0.0 copy-start.1
  184.0 0.0 collective-permute-done.1.refs_4_
  184.0 2.3 copy-done.1
  186.3 80.0 %combine.1 = f32[256,128]{1,0:T(8,128)} custom-call(bf16[10368,256]{1,0:T(8,128)(2,1)} %get-tuple-element.9.f_ref.refs_0_, bf16[10368,256]{1,0:T(8,128)(2,1)} %get-tuple-element.10.next_ref.refs_1_, bf16[10368,256]{1,0:T(8,128)(2,1)} %copy-done.1, bf16[10368,256]{1,0:T(8,128)(2,1)} %get-tuple-element.11.w_ref.refs_3_, ...), custom_call_target="tpu_custom_call" | custom-call | tf_op jit(solution)/shard_map/combine/pallas_call | solution.py:474
  266.3 1.6 copy.41
  (4 shorter events, 0.1 us)
Async XLA Ops:
  0.6 8.5 %copy-start = (bf16[512,512]{1,0:T(8,128)(2,1)S(1)}, bf16[512,512]{1,0:T(8,128)(2,1)}, u32[]{:S(2)}) copy-start(bf16[512,512]{1,0:T(8,128)(2,1)} %param.9) | copy-start | bytes 1572868
  0.6 7.1 %copy-start.2 = (f32[10368]{0:T(1024)S(1)}, f32[10368]{0:T(1024)}, u32[]{:S(2)}) copy-start(f32[10368]{0:T(1024)} %param.8) | copy-start | bytes 124420
  154.3 29.7 %collective-permute-start = (bf16[10368,256]{1,0:T(8,128)(2,1)}, bf16[10368,256]{1,0:T(8,128)(2,1)S(1)}, u32[]{:S(2)}, u32[]{:S(2)}) collective-permute-start(bf16[10368,256]{1,0:T(8,128)(2,1)} %get-tuple-element.10.next_ref.refs_1_), channel_id=1, source_target_pairs={{1,2},{6,5},{9,10},{14,13},{17,18},{22,21},{25,26},{30,29}} | collective-permute-start | bytes 15925256 | tf_op jit(solution)/shard_map/ppermute | solution.py:447
  155.3 28.7 %collective-permute-start.1 = (bf16[10368,256]{1,0:T(8,128)(2,1)}, bf16[10368,256]{1,0:T(8,128)(2,1)}, u32[]{:S(2)}, u32[]{:S(2)}) collective-permute-start(bf16[10368,256]{1,0:T(8,128)(2,1)} %get-tuple-element.11.w_ref.refs_3_), channel_id=1, source_target_pairs={{3,2},{4,5},{11,10},{12,13},{19,18},{20,21},{27,26},{28,29}} | collective-permute-start | bytes 15925256 | tf_op jit(solution)/shard_map/ppermute | solution.py:447
  184.0 2.3 copy-start.1
